TPU v7x, 32 devices: a whole 2x2x4 slice. The times are simulated.
32 devices in a mesh: ctx: 16 (over z, y, x), shard: 2 (over core).
Axes of the slice: x: 2, y: 2, z: 4, core: 2. Of those that a mesh axis runs over, the one named last changes fastest.
Arguments:
- inputs: bfloat16 [2, 4608, 768], P('shard', 'ctx'), may hold values from -6 to 6
- cotangent: bfloat16 [2, 4608, 768], P('shard', 'ctx'), may hold values from -6 to 6
- block_table: int32 [16, 2], replicated, may hold values from 0 to 31, as said below
- first_gain: bfloat16 [768], P('shard'), may hold values from 0.5 to 1.5
- first_shift: bfloat16 [768], P('shard'), may hold values from -0.59765625 to 0.59765625
- query_weight: bfloat16 [768, 768], P('shard'), may hold values from -0.4375 to 0.4375
- query_bias: bfloat16 [768], P('shard'), may hold values from -0.59765625 to 0.59765625
- keyvalue_weight: bfloat16 [768, 1536], P('shard'), may hold values from -0.21875 to 0.21875
- value_bias: bfloat16 [768], P('shard'), may hold values from -0.29882812 to 0.29882812
- out_weight: bfloat16 [768, 768], P('shard'), may hold values from -1.75 to 1.75
- out_bias: bfloat16 [768], P('shard'), may hold values from -0.59765625 to 0.59765625
- second_gain: bfloat16 [768], P('shard'), may hold values from 0.5 to 1.5
- second_shift: bfloat16 [768], P('shard'), may hold values from -0.59765625 to 0.59765625
- up_weight: bfloat16 [768, 3072], P('shard'), may hold values from -0.21875 to 0.21875
- up_bias: bfloat16 [3072], P('shard'), may hold values from -0.59765625 to 0.59765625
- down_weight: bfloat16 [3072, 768], P('shard'), may hold values from -0.109375 to 0.109375
- down_bias: bfloat16 [768], P('shard'), may hold values from -0.59765625 to 0.59765625
Outputs:
- outputs: bfloat16 [2, 4608, 768], P('shard', 'ctx')
- input_grad: bfloat16 [2, 4608, 768], P('shard', 'ctx')
- first_gain_grad: float32 [768], P('shard')
- first_shift_grad: float32 [768], P('shard')
- query_weight_grad: float32 [768, 768], P('shard')
- query_bias_grad: float32 [768], P('shard')
- keyvalue_weight_grad: float32 [768, 1536], P('shard')
- value_bias_grad: float32 [768], P('shard')
- out_weight_grad: float32 [768, 768], P('shard')
- out_bias_grad: float32 [768], P('shard')
- second_gain_grad: float32 [768], P('shard')
- second_shift_grad: float32 [768], P('shard')
- up_weight_grad: float32 [768, 3072], P('shard')
- up_bias_grad: float32 [3072], P('shard')
- down_weight_grad: float32 [3072, 768], P('shard')
- down_bias_grad: float32 [768], P('shard')
Inputs may be any that keep to these rules, and one draw needn't show every extreme that they name: `block_table`: row d holds a block number b and its mirror 32 - 1 - b, in either order; every block number stands once in the table.
All inputs are finite; a program needn't handle non-finite values.
Results may differ from a plain program's by a relative error of at most 0.017.
Values may be sent and summed in bfloat16 or wider, within the bound.
A program may use at most 512 MiB of HBM per device.

v0:
```python
import jax
import jax.numpy as jnp
from jax import lax
from jax.sharding import PartitionSpec as P

HD = 64


EPSILON = 1e-05
NEGATIVE = -1e30


def shortened(shard):

    def short(part):
        return part.astype(jnp.bfloat16) if part.dtype == jnp.float32 else part

    return jax.tree.map(short, shard)


def normalize(values, gain, shift):
    centre = values - jnp.mean(values, -1, keepdims=True)
    spread = jnp.mean(centre * centre, -1, keepdims=True)
    return centre * lax.rsqrt(spread + EPSILON) * gain + shift


def gelu_tanh(values):
    return jax.nn.gelu(values, approximate=True)


def matmul(left, right):
    return jnp.dot(left, right, preferred_element_type=jnp.float32)


def outer_sum(left, right):
    return lax.dot_general(
        left, right, (((0,), (0,)), ((), ())), preferred_element_type=jnp.float32
    )


def times_transpose(left, right):
    return lax.dot_general(
        left, right, (((1,), (1,)), ((), ())), preferred_element_type=jnp.float32
    )


def fetch_tile(blocks, inverse, first_block, tile_blocks):
    picks = lax.dynamic_slice_in_dim(inverse, first_block, tile_blocks, 0)
    chosen = jnp.take(blocks, picks, axis=0)
    return chosen.reshape((chosen.shape[0] * chosen.shape[1],) + chosen.shape[2:])


def scores_against(query_rows, query_places, kv_blocks, inverse, tile_blocks, step):
    block_rows, head_count, head_size = query_rows.shape
    tile_rows = block_rows * tile_blocks
    key_tile = fetch_tile(kv_blocks, inverse, step * tile_blocks, tile_blocks)
    key_tile = key_tile.reshape(tile_rows, 2, head_count, head_size)
    scores = jnp.einsum(
        "qhd,khd->hqk", query_rows, key_tile[:, 0], preferred_element_type=jnp.float32
    )
    key_places = step * tile_rows + jnp.arange(tile_rows, dtype=jnp.int32)
    allowed = (query_places[:, None] >= key_places[None, :])[None]
    return (key_tile, allowed, jnp.where(allowed, scores, NEGATIVE))


def attend_rows(query_rows, first_row, kv_blocks, inverse, tile_blocks):
    block_rows, head_count, head_size = query_rows.shape
    tile_rows = block_rows * tile_blocks
    trip_count = first_row // tile_rows + 1
    query_places = first_row + jnp.arange(block_rows, dtype=jnp.int32)

    def stats_step(step, carry):
        running, denominator = carry
        _, _, scores = scores_against(
            query_rows, query_places, kv_blocks, inverse, tile_blocks, step
        )
        new_running = jnp.maximum(running, jnp.max(scores, -1))
        denominator = denominator * jnp.exp(running - new_running) + jnp.sum(
            jnp.exp(scores - new_running[:, :, None]), -1
        )
        return (new_running, denominator)

    start_stats = (
        jnp.full((head_count, block_rows), NEGATIVE, jnp.float32),
        jnp.zeros((head_count, block_rows), jnp.float32),
    )
    running, denominator = lax.fori_loop(0, trip_count, stats_step, start_stats)
    log_total = running + jnp.log(denominator)

    def value_step(step, partial_value):
        key_tile, allowed, scores = scores_against(
            query_rows, query_places, kv_blocks, inverse, tile_blocks, step
        )
        chances = jnp.where(allowed, jnp.exp(scores - log_total[:, :, None]), 0.0).astype(
            jnp.bfloat16
        )
        return partial_value + jnp.einsum(
            "hqk,khd->qhd", chances, key_tile[:, 1], preferred_element_type=jnp.float32
        )

    attended = lax.fori_loop(
        0, trip_count, value_step, jnp.zeros((block_rows, head_count, head_size), jnp.float32)
    )
    return (attended, log_total)


def query_grads(
    query_rows, grad_rows, first_row, log_total, delta, kv_blocks, inverse, tile_blocks, kv_sums
):
    block_rows, head_count, head_size = query_rows.shape
    tile_rows = block_rows * tile_blocks
    trip_count = first_row // tile_rows + 1
    query_places = first_row + jnp.arange(block_rows, dtype=jnp.int32)

    def grad_step(step, carry):
        query_grad, partial_value = carry
        key_tile, allowed, scores = scores_against(
            query_rows, query_places, kv_blocks, inverse, tile_blocks, step
        )
        chances = jnp.where(allowed, jnp.exp(scores - log_total[:, :, None]), 0.0)
        dchance = jnp.einsum(
            "qhd,khd->hqk", grad_rows, key_tile[:, 1], preferred_element_type=jnp.float32
        )
        dscores = (chances * (dchance - delta[:, :, None])).astype(jnp.bfloat16)
        query_grad = query_grad + jnp.einsum(
            "hqk,khd->qhd", dscores, key_tile[:, 0], preferred_element_type=jnp.float32
        )
        key_grad = jnp.einsum(
            "hqk,qhd->khd", dscores, query_rows, preferred_element_type=jnp.float32
        )
        value_grad = jnp.einsum(
            "hqk,qhd->khd",
            chances.astype(jnp.bfloat16),
            grad_rows,
            preferred_element_type=jnp.float32,
        )
        both = jnp.stack([key_grad, value_grad], 1).reshape(
            tile_blocks, block_rows, 2, head_count * head_size
        )
        picks = lax.dynamic_slice_in_dim(inverse, step * tile_blocks, tile_blocks, 0)
        partial_value = partial_value.at[picks].add(both)
        return (query_grad, partial_value)

    start_grad = jnp.zeros((block_rows, head_count, head_size), jnp.float32)
    return lax.fori_loop(0, trip_count, grad_step, (start_grad, kv_sums))


def add_terms(terms):
    return tuple((term_part for term_part in terms))


def body(
    inputs,
    cotangent,
    block_table,
    first_gain,
    first_shift,
    query_weight,
    query_bias,
    keyvalue_weight,
    value_bias,
    out_weight,
    out_bias,
    second_gain,
    second_shift,
    up_weight,
    up_bias,
    down_weight,
    down_bias,
):
    ctx_count = lax.axis_size("ctx")
    my_index = lax.axis_index("ctx")
    seq_here, local_rows, model_width = inputs.shape
    block_rows = local_rows // 2
    head_count = model_width // HD
    tile_blocks = min(16, 2 * ctx_count)
    dealt_order = block_table.reshape(-1)
    inverse = jnp.argsort(dealt_order)
    my_blocks = lax.dynamic_index_in_dim(block_table, my_index, 0, keepdims=False)
    gathered = (
        lax.all_gather(first_gain, "shard", axis=0, tiled=True),
        lax.all_gather(first_shift, "shard", axis=0, tiled=True),
        lax.all_gather(query_weight, "shard", axis=0, tiled=True),
        lax.all_gather(query_bias, "shard", axis=0, tiled=True),
        lax.all_gather(keyvalue_weight, "shard", axis=0, tiled=True),
        lax.all_gather(value_bias, "shard", axis=0, tiled=True),
        lax.all_gather(out_weight, "shard", axis=0, tiled=True),
        lax.all_gather(out_bias, "shard", axis=0, tiled=True),
        lax.all_gather(second_gain, "shard", axis=0, tiled=True),
        lax.all_gather(second_shift, "shard", axis=0, tiled=True),
        lax.all_gather(up_weight, "shard", axis=0, tiled=True),
        lax.all_gather(up_bias, "shard", axis=0, tiled=True),
        lax.all_gather(down_weight, "shard", axis=0, tiled=True),
        lax.all_gather(down_bias, "shard", axis=0, tiled=True),
    )
    (
        gain_one,
        shift_one,
        w_query,
        b_query,
        w_keyvalue,
        b_value,
        w_out,
        b_out,
        gain_two,
        shift_two,
        w_up,
        b_up,
        w_down,
        b_down,
    ) = gathered
    gain_one = gain_one.astype(jnp.float32)
    shift_one = shift_one.astype(jnp.float32)
    gain_two = gain_two.astype(jnp.float32)
    shift_two = shift_two.astype(jnp.float32)
    b_query = b_query.astype(jnp.float32)
    b_out = b_out.astype(jnp.float32)
    b_up = b_up.astype(jnp.float32)
    b_down = b_down.astype(jnp.float32)
    value_shift = b_value.astype(jnp.float32)
    kv_shift = jnp.concatenate([jnp.zeros_like(value_shift), value_shift])
    totals = tuple((jnp.zeros(param_part.shape, jnp.float32) for param_part in gathered))
    hidden = inputs[0].astype(jnp.float32)
    normed = normalize(hidden, gain_one, shift_one).astype(jnp.bfloat16)
    queries = ((matmul(normed, w_query) + b_query) * 0.125).astype(jnp.bfloat16)
    kv_local = (
        (matmul(normed, w_keyvalue) + kv_shift)
        .astype(jnp.bfloat16)
        .reshape(local_rows, 2, model_width)
    )
    kv_all = lax.all_gather(kv_local, "ctx", axis=0, tiled=True)
    kv_blocks = kv_all.reshape(2 * ctx_count, block_rows, 2, model_width)
    query_heads = queries.reshape(2, block_rows, head_count, HD)
    first_rows = my_blocks * block_rows
    attended_a, log_total_a = attend_rows(
        query_heads[0], first_rows[0], kv_blocks, inverse, tile_blocks
    )
    attended_b, log_total_b = attend_rows(
        query_heads[1], first_rows[1], kv_blocks, inverse, tile_blocks
    )
    attended = jnp.concatenate([attended_a, attended_b], 0)
    attended_low = attended.reshape(local_rows, model_width).astype(jnp.bfloat16)
    middle = hidden + matmul(attended_low, w_out) + b_out
    second = normalize(middle, gain_two, shift_two).astype(jnp.bfloat16)
    pre_act = matmul(second, w_up) + b_up
    active = gelu_tanh(pre_act).astype(jnp.bfloat16)
    result = middle + matmul(active, w_down) + b_down
    output_list = [result.astype(jnp.bfloat16)]
    upstream = cotangent[0].astype(jnp.float32)
    down_grad_in = upstream.astype(jnp.bfloat16)
    dactive = times_transpose(down_grad_in, w_down)
    _, gelu_pull = jax.vjp(gelu_tanh, pre_act)
    dpre = gelu_pull(dactive)[0].astype(jnp.bfloat16)
    dsecond = times_transpose(dpre, w_up)
    _, norm_pull_two = jax.vjp(normalize, middle, gain_two, shift_two)
    dmiddle_part, dgain_two, dshift_two = norm_pull_two(dsecond)
    dmiddle = upstream + dmiddle_part
    dbranch = dmiddle.astype(jnp.bfloat16)
    dattended = times_transpose(dbranch, w_out).astype(jnp.bfloat16)
    delta = jnp.sum(
        dattended.astype(jnp.float32).reshape(local_rows, head_count, HD) * attended, -1
    )
    delta_blocks = delta.reshape(2, block_rows, head_count)
    dattended_heads = dattended.reshape(2, block_rows, head_count, HD)
    kv_sums = jnp.zeros((2 * ctx_count, block_rows, 2, model_width), jnp.float32)
    dquery_a, kv_sums = query_grads(
        query_heads[0],
        dattended_heads[0],
        first_rows[0],
        log_total_a,
        jnp.transpose(delta_blocks[0]),
        kv_blocks,
        inverse,
        tile_blocks,
        kv_sums,
    )
    dquery_b, kv_sums = query_grads(
        query_heads[1],
        dattended_heads[1],
        first_rows[1],
        log_total_b,
        jnp.transpose(delta_blocks[1]),
        kv_blocks,
        inverse,
        tile_blocks,
        kv_sums,
    )
    kv_grad = lax.psum_scatter(
        kv_sums.reshape(2 * ctx_count * block_rows, 2, model_width),
        "ctx",
        scatter_dimension=0,
        tiled=True,
    )
    kv_grad_low = kv_grad.astype(jnp.bfloat16).reshape(local_rows, 2 * model_width)
    dquery = (
        jnp.concatenate([dquery_a, dquery_b], 0)
        .reshape(local_rows, model_width)
        .astype(jnp.bfloat16)
    )
    dnormed = times_transpose(dquery, w_query) * 0.125 + times_transpose(kv_grad_low, w_keyvalue)
    _, norm_pull_one = jax.vjp(normalize, hidden, gain_one, shift_one)
    dhidden_part, dgain_one, dshift_one = norm_pull_one(dnormed)
    grad_list = [(dmiddle + dhidden_part).astype(jnp.bfloat16)]
    kv_grad_wide = kv_grad_low.astype(jnp.float32)
    terms = (
        dgain_one,
        dshift_one,
        outer_sum(normed, dquery) * 0.125,
        jnp.sum(dquery.astype(jnp.float32), 0) * 0.125,
        outer_sum(normed, kv_grad_low),
        jnp.sum(kv_grad_wide[:, model_width:], 0),
        outer_sum(attended_low, dbranch),
        jnp.sum(dbranch.astype(jnp.float32), 0),
        dgain_two,
        dshift_two,
        outer_sum(second, dpre),
        jnp.sum(dpre.astype(jnp.float32), 0),
        outer_sum(active, down_grad_in),
        jnp.sum(down_grad_in.astype(jnp.float32), 0),
    )
    totals = add_terms(terms)
    summed = lax.psum(totals, "ctx")
    shares = jax.tree.map(
        lambda part: part.astype(jnp.float32),
        lax.psum_scatter(shortened(summed), "shard", scatter_dimension=0, tiled=True),
    )
    return (jnp.stack(output_list), jnp.stack(grad_list)) + tuple(shares)


def solution(mesh):
    in_specs = (
        P("shard", "ctx", None),
        P("shard", "ctx", None),
        P(),
        P("shard"),
        P("shard"),
        P("shard", None),
        P("shard"),
        P("shard", None),
        P("shard"),
        P("shard", None),
        P("shard"),
        P("shard"),
        P("shard"),
        P("shard", None),
        P("shard"),
        P("shard", None),
        P("shard"),
    )
    out_specs = (
        P("shard", "ctx", None),
        P("shard", "ctx", None),
        P("shard"),
        P("shard"),
        P("shard", None),
        P("shard"),
        P("shard", None),
        P("shard"),
        P("shard", None),
        P("shard"),
        P("shard"),
        P("shard"),
        P("shard", None),
        P("shard"),
        P("shard", None),
        P("shard"),
    )
    return jax.shard_map(body, mesh=mesh, in_specs=in_specs, out_specs=out_specs, check_vma=False)
```

profile of v0, /device:TPU:0, one launch (start us, length us, event | category | flops | bytes accessed | tf_op | source)
XLA Modules:
  0.0 3118.8 jit_solution(4978161835801098211)
XLA Ops:
  49.9 156.8 %all-gather.18.cloned.1.call-done = bf16[4608,2,768]{2,1,0:T(2,128)(2,1)} async-done(((bf16[288,2,768]{2,1,0:T(2,128)(2,1)}), bf16[4608,2,768]{2,1,0:T(2,128)(2,1)}) %all-gather.18.cloned.1.call-update) | async-done | bytes 14155792 | tf_op jit(solution)/shard_map/all_gather | solution.py:231
  206.7 94.2 %while.76 = (s32[]{:T(128)}, f32[12,144]{1,0:T(8,128)S(1)}, f32[12,144]{1,0:T(8,128)S(1)}, s32[]{:T(128)}, s32[32]{0:T(128)S(1)}, /*index=5*/bf16[32,144,2,768]{...) while((s32[]{:T(128)}, f32[12,144]{1,0:T(8,128)S(1)}, ...), condition=%wide.region_12.14_spmd.clone, body=%wide.region_9.13_spmd.clone.sunk | while | flops 533392256 | bytes 93343080 | solution.py:87
  208.0 21.4 gather_fusion.2
  239.3 21.3 copy.111
  301.0 82.5 %while.77 = (s32[]{:T(128)}, f32[144,12,64]{0,2,1:T(8,128)S(1)}, s32[]{:T(128)}, s32[32]{0:T(128)S(1)}, bf16[32,144,2,768]{3,2,1,0:T(2,128)(2,1)}, /*index=5*/bf...) while((s32[]{:T(128)}, f32[144,12,64]{0,2,1:T(8,128)S(1)}, ...), condition=%wide.region_14.16_spmd.clone, body=%wide.region_13.15_spmd.clone.sunk | while | flops 1039126016 | bytes 65501544 | solution.py:101
  302.1 21.2 gather_fusion.3
  385.1 185.8 %while.74 = (s32[]{:T(128)}, f32[12,144]{1,0:T(8,128)S(1)}, f32[12,144]{1,0:T(8,128)S(1)}, s32[]{:T(128)}, s32[32]{0:T(128)S(1)}, /*index=5*/bf16[32,144,2,768]{...) while((s32[]{:T(128)}, f32[12,144]{1,0:T(8,128)S(1)}, ...), condition=%wide.region_6.8_spmd.clone, body=%wide.region_3.7_spmd.clone.sunk | while | flops 533392256 | bytes 93343080 | solution.py:87
  386.3 21.2 gather_fusion
  479.0 21.2 gather_fusion
  571.0 165.4 %while.75 = (s32[]{:T(128)}, f32[144,12,64]{0,2,1:T(8,128)S(1)}, s32[]{:T(128)}, s32[32]{0:T(128)S(1)}, bf16[32,144,2,768]{3,2,1,0:T(2,128)(2,1)}, /*index=5*/bf...) while((s32[]{:T(128)}, f32[144,12,64]{0,2,1:T(8,128)S(1)}, ...), condition=%wide.region_8.10_spmd.clone, body=%wide.region_7.9_spmd.clone.sunk | while | flops 1039126016 | bytes 65501544 | solution.py:101
  572.2 21.2 gather_fusion.1
  654.6 21.2 gather_fusion.1
  774.8 452.2 %while.78 = (s32[]{:T(128)}, f32[144,12,64]{0,2,1:T(8,128)S(1)}, f32[32,144,2,768]{3,1,2,0:T(8,128)}, s32[]{:T(128)}, s32[32]{0:T(128)S(1)}, /*index=5*/bf16[32,...) while((s32[]{:T(128)}, f32[144,12,64]{0,2,1:T(8,128)S(1)}, ...), condition=%wide.region_22.24_spmd.clone, body=%wide.region_20.23_spmd.clone.sunk | while | flops 2598915584 | bytes 315121600 | solution.py:145
  775.1 21.2 gather_fusion.4
  941.2 21.5 copy.114
  962.7 30.7 scatter_fusion
  993.5 21.2 gather_fusion.4
  1159.6 21.5 copy.114
  1181.0 31.0 scatter_fusion
  1228.0 218.8 %while.79 = (s32[]{:T(128)}, f32[144,12,64]{0,2,1:T(8,128)S(1)}, f32[32,144,2,768]{3,1,2,0:T(8,128)}, s32[]{:T(128)}, s32[32]{0:T(128)S(1)}, /*index=5*/bf16[32,...) while((s32[]{:T(128)}, f32[144,12,64]{0,2,1:T(8,128)S(1)}, ...), condition=%wide.region_25.27_spmd.clone, body=%wide.region_23.26_spmd.clone.sunk | while | flops 2598915584 | bytes 315121600 | solution.py:145
  1394.2 21.5 copy.116
  1415.6 30.7 scatter_fusion.1
  1489.1 374.1 %reduce-scatter.7.cloned.1.call-done = f32[288,2,768]{2,0,1:T(8,128)} async-done(((f32[4608,2,768]{2,0,1:T(8,128)}), f32[288,2,768]{2,0,1:T(8,128)}) %reduce-scatter.7.cloned.1.call-update) | async-done | bytes 1769488 | tf_op jit(solution)/shard_map/reduce_scatter | solution.py:288
  1871.7 1160.9 %all-reduce.13 = (bf16[768]{0:T(1024)(128)(2,1)S(1)}, bf16[768]{0:T(1024)(128)(2,1)S(1)}, bf16[768,768]{1,0:T(8,128)(2,1)}, bf16[768]{0:T(1024)(128)(2,1)S(1)}, ...) all-reduce(f32[768]{0:T(1024)S(1)} %get-tuple-element.509, ...), channel_id=1, replica_groups=mesh['ctx'=16,'shard'=2] {'ctx'}, use_global_device_ids=true, to_apply=%region_30.32 | all-reduce | flops 7087104 | bytes 42522624 | tf_op jit(solution)/shard_map/psum | solution.py:322
  (408 shorter events, 1041.0 us)
Async XLA Ops:
  7.2 16.1 all-gather.16.cloned.1.call-start
  7.9 38.9 %all-gather.20.cloned.1.call-start = ((), (), s32[]{:S(2)}) async-start(), calls=%async_computation.8 | async-start | bytes 1769472 | tf_op jit(solution)/shard_map/all_gather | solution.py:183
  8.7 198.0 %all-gather.18.cloned.1.call-start = ((), (), s32[]{:S(2)}) async-start(), calls=%async_computation.7 | async-start | bytes 15040512 | tf_op jit(solution)/shard_map/all_gather | solution.py:231
  27.2 709.6 %all-gather.22.cloned.1.call-start = ((), (), s32[]{:S(2)}) async-start(), calls=%async_computation.9 | async-start | bytes 1769472 | tf_op jit(solution)/shard_map/all_gather | solution.py:187
  27.7 711.9 %all-gather.24.cloned.1.call-start = ((), (), s32[]{:S(2)}) async-start(), calls=%async_computation.10 | async-start | bytes 7077888 | tf_op jit(solution)/shard_map/all_gather | solution.py:191
  28.3 717.2 %all-gather.26.cloned.1.call-start = ((), (), s32[]{:S(2)}) async-start(), calls=%async_computation.11 | async-start | bytes 7077888 | tf_op jit(solution)/shard_map/all_gather | solution.py:193
  28.9 1834.3 %reduce-scatter.7.cloned.1.call-start = ((), (), s32[]{:S(2)}) async-start(), calls=%async_computation.12 | async-start | bytes 30081024 | tf_op jit(solution)/shard_map/reduce_scatter | solution.py:288
  301.0 83.2 %copy-start.4 = (bf16[144,768]{0,1:T(8,128)(2,1)S(1)}, bf16[144,768]{0,1:T(8,128)(2,1)}, u32[]{:S(2)}) copy-start(bf16[144,768]{0,1:T(8,128)(2,1)} %copy.93) | copy-start | bytes 663556
  571.0 165.5 %copy-start.15 = (f32[144,12,64]{0,2,1:T(8,128)S(1)}, f32[144,12,64]{0,2,1:T(8,128)}, u32[]{:S(2)}) copy-start(f32[144,12,64]{0,2,1:T(8,128)} %copy-done.14) | copy-start | bytes 1327108
  571.0 166.4 %copy-start.8 = (bf16[1,288,768]{2,1,0:T(8,128)(2,1)S(1)}, bf16[1,288,768]{2,1,0:T(8,128)(2,1)}, u32[]{:S(2)}) copy-start(bf16[1,288,768]{2,1,0:T(8,128)(2,1)} %param.31) | copy-start | bytes 1327108
  571.0 166.4 %copy-start.57 = (f32[768]{0:T(1024)S(1)}, f32[768]{0:T(1024)}, u32[]{:S(2)}) copy-start(f32[768]{0:T(1024)} %reshape.529) | copy-start | bytes 9220
  571.0 168.6 %copy-start.29 = (f32[768]{0:T(1024)S(1)}, f32[768]{0:T(1024)}, u32[]{:S(2)}) copy-start(f32[768]{0:T(1024)} %reshape.530) | copy-start | bytes 9220
  571.0 168.6 %copy-start.33 = (f32[768]{0:T(1024)S(1)}, f32[768]{0:T(1024)}, u32[]{:S(2)}) copy-start(f32[768]{0:T(1024)} %reshape.531) | copy-start | bytes 9220
  571.0 168.6 %copy-start.54 = (f32[2,1,1536]{2,1,0:T(1,128)S(1)}, f32[2,1,1536]{2,1,0:T(1,128)}, u32[]{:S(2)}) copy-start(f32[2,1,1536]{2,1,0:T(1,128)} %convert_element_type.271) | copy-start | bytes 36868
  774.8 452.2 %copy-start.25 = (bf16[144,768]{1,0:T(8,128)(2,1)S(1)}, bf16[144,768]{1,0:T(8,128)(2,1)}, u32[]{:S(2)}) copy-start(bf16[144,768]{1,0:T(8,128)(2,1)} %get-tuple-element.669) | copy-start | bytes 663556
  774.8 453.2 %copy-start.3 = (bf16[144,12,64]{0,2,1:T(8,128)(2,1)S(1)}, bf16[144,12,64]{0,2,1:T(8,128)(2,1)}, u32[]{:S(2)}) copy-start(bf16[144,12,64]{0,2,1:T(8,128)(2,1)} %copy-done.2) | copy-start | bytes 663556
  774.8 453.2 %copy-start.49 = (f32[12,144]{1,0:T(8,128)S(1)}, f32[12,144]{1,0:T(8,128)}, u32[]{:S(2)}) copy-start(f32[12,144]{1,0:T(8,128)} %copy-done.48) | copy-start | bytes 20740
  774.8 453.2 %copy-start.52 = (f32[12,144]{1,0:T(8,128)S(1)}, f32[12,144]{1,0:T(8,128)}, u32[]{:S(2)}) copy-start(f32[12,144]{1,0:T(8,128)} %get-tuple-element.1265) | copy-start | bytes 20740
  1466.8 1588.0 %reduce-scatter.9.cloned.1.call-start = ((), (), s32[]{:S(2)}) async-start(), calls=%async_computation.13 | async-start | bytes 1769472 | tf_op jit(solution)/shard_map/reduce_scatter | solution.py:325
  1489.1 379.7 %copy-start.26 = (f32[288,768]{1,0:T(8,128)S(1)}, f32[288,768]{1,0:T(8,128)}, u32[]{:S(2)}) copy-start(f32[288,768]{1,0:T(8,128)} %convolution_multiply_fusion.1) | copy-start | bytes 2654212
  3032.6 29.0 reduce-scatter.13.cloned.1.call-start
  3033.4 41.5 %reduce-scatter.11.cloned.1.call-start = ((), (), s32[]{:S(2)}) async-start(), calls=%async_computation.14 | async-start | bytes 3538944 | tf_op jit(solution)/shard_map/reduce_scatter | solution.py:325
  3034.0 57.7 %reduce-scatter.15.cloned.1.call-start = ((), (), s32[]{:S(2)}) async-start(), calls=%async_computation.16 | async-start | bytes 7077888 | tf_op jit(solution)/shard_map/reduce_scatter | solution.py:325
  3034.7 72.9 %reduce-scatter.17.cloned.1.call-start = ((), (), s32[]{:S(2)}) async-start(), calls=%async_computation.17 | async-start | bytes 7077888 | tf_op jit(solution)/shard_map/reduce_scatter | solution.py:325
  (59 other events, 474.3 us)
Sparse Core Ops, SparseCore 0:
  9.6 13.6 all-gather.15
  24.8 10.3 all-gather.19
  38.6 168.0 all-gather.17
  208.1 7.4 all-gather.21
  216.9 15.5 all-gather.23
  234.0 15.6 all-gather.25
  1466.9 396.2 reduce-scatter.6
  3032.8 16.5 reduce-scatter.8
  3051.7 9.8 reduce-scatter.12
  3063.7 11.1 reduce-scatter.10
  3077.8 13.7 reduce-scatter.14
  3093.8 13.7 reduce-scatter.16
where the time goes:
time: 3140 us; the launch traced here: 3120 us
  blocking collectives  1180 us (38%)
  local copies, waits for them, and re-layouts  772 us (25%)
  waiting for transfers between devices  581 us (19%)
  other arithmetic  304 us (10%)
  matrix products  243 us (8%)
    psum x1, blocking collectives, body(): summed = lax.psum(totals, 'ctx')  1160 us
    reduce_scatter x1, waiting for transfers between devices, body(): lax.psum_scatter(kv_sums.reshape(2 * ctx_count * block_rows, 2, model_wid...  374 us
    gather x9, local copies, waits for them, and re-layouts, fetch_tile(): chosen = jnp.take(blocks, picks, axis=0)  191 us
    reshape x9, local copies, waits for them, and re-layouts, scores_against(): key_tile = key_tile.reshape(tile_rows, 2, head_count, head_size)  188 us
    select_n x9, local copies, waits for them, and re-layouts, fetch_tile(): chosen = jnp.take(blocks, picks, axis=0)  188 us
    all_gather x1, waiting for transfers between devices, body(): kv_all = lax.all_gather(kv_local, 'ctx', axis=0, tiled=True)  157 us
    another operation x9, local copies, waits for them, and re-layouts, grad_step(): jnp.stack([key_grad, value_grad], 1)  147 us
    scatter-add x3, other arithmetic, grad_step(): partial_value = partial_value.at[picks].add(both)  92.4 us
  transfers between devices with their start and end apart: 12, of which 7 were waited for; matrix products, arithmetic and copies ran while one was open for 19% of the time, Pallas kernels for 0%

commit v1 on v0

v1 whole, which is shorter than its diff:
```python
import jax
import jax.numpy as jnp
from jax import lax
from jax.experimental import pallas as pl
from jax.experimental.pallas import tpu as pltpu
from jax.sharding import PartitionSpec as P

HD = 64


EPSILON = 1e-05
NEGATIVE = -1e30


def normalize(values, gain, shift):
    centre = values - jnp.mean(values, -1, keepdims=True)
    spread = jnp.mean(centre * centre, -1, keepdims=True)
    return centre * lax.rsqrt(spread + EPSILON) * gain + shift


def gelu_tanh(values):
    return jax.nn.gelu(values, approximate=True)


def matmul(left, right):
    return jnp.dot(left, right, preferred_element_type=jnp.float32)


def outer_sum(left, right):
    return lax.dot_general(
        left, right, (((0,), (0,)), ((), ())), preferred_element_type=jnp.float32
    )


def times_transpose(left, right):
    return lax.dot_general(
        left, right, (((1,), (1,)), ((), ())), preferred_element_type=jnp.float32
    )


def key_tile_rows(length):
    for rows in (512, 384, 256, 128):
        if length % rows == 0:
            return rows
    return length


def head_halves(rows):
    block_rows, lanes = rows.shape
    lane = lax.broadcasted_iota(jnp.int32, (block_rows, lanes), 1)
    low_mask = (lane < HD).astype(jnp.float32).astype(rows.dtype)
    high_mask = (lane >= HD).astype(jnp.float32).astype(rows.dtype)
    return jnp.concatenate([rows * low_mask, rows * high_mask], 0)


def join_halves(both):
    block_rows = both.shape[0] // 2
    lane = lax.broadcasted_iota(jnp.int32, (block_rows, both.shape[1]), 1)
    return jnp.where(lane < HD, both[:block_rows], both[block_rows:])


def to_sequence(table, block_rows, pairs):
    def move(slot, _):
        source = pl.ds(pl.multiple_of(slot * block_rows, block_rows), block_rows)
        target = pl.ds(pl.multiple_of(table[slot] * block_rows, block_rows), block_rows)
        for dealt, ordered in pairs:
            ordered[target, :] = dealt[source, :]
        return 0

    lax.fori_loop(0, table.shape[0], move, 0)


def allowed_mask(first, block_rows, tile, tile_rows):
    shape = (2 * block_rows, tile_rows)
    row = lax.broadcasted_iota(jnp.int32, shape, 0)
    row = jnp.where(row >= block_rows, row - block_rows, row)
    col = lax.broadcasted_iota(jnp.int32, shape, 1)
    return row - col >= tile * tile_rows - first


def forward_kernel(table, mine, q_ref, k_ref, v_ref, o_ref, lse_ref, k_seq, v_seq):
    block_rows = q_ref.shape[0] // 2
    tile_rows = key_tile_rows(k_ref.shape[0])
    to_sequence(table, block_rows, ((k_ref, k_seq), (v_ref, v_seq)))
    for half in range(2):
        rows = pl.ds(half * block_rows, block_rows)
        queries = head_halves(q_ref[rows, :])
        first = mine[half] * block_rows

        def step(tile, carry, masked):
            running, denominator, total = carry
            place = pl.ds(pl.multiple_of(tile * tile_rows, tile_rows), tile_rows)
            scores = times_transpose(queries, k_seq[place, :])
            if masked:
                scores = jnp.where(
                    allowed_mask(first, block_rows, tile, tile_rows), scores, NEGATIVE
                )
            new_running = jnp.maximum(running, jnp.max(scores, -1, keepdims=True))
            decay = jnp.exp(running - new_running)
            chances = jnp.exp(scores - new_running)
            denominator = denominator * decay + jnp.sum(chances, -1, keepdims=True)
            total = total * decay + matmul(chances.astype(jnp.bfloat16), v_seq[place, :])
            return new_running, denominator, total

        start = (
            jnp.full((2 * block_rows, 1), NEGATIVE, jnp.float32),
            jnp.zeros((2 * block_rows, 1), jnp.float32),
            jnp.zeros((2 * block_rows, q_ref.shape[1]), jnp.float32),
        )
        full = (first + 1) // tile_rows
        count = (first + block_rows - 1) // tile_rows + 1
        carry = lax.fori_loop(0, full, lambda t, c: step(t, c, False), start)
        running, denominator, total = lax.fori_loop(
            full, count, lambda t, c: step(t, c, True), carry
        )
        o_ref[rows, :] = join_halves(total / denominator)
        lse_ref[0, pl.ds(half * 2 * block_rows, 2 * block_rows), :] = jnp.broadcast_to(
            running + jnp.log(denominator), (2 * block_rows, lse_ref.shape[2])
        )


def backward_kernel(
    table, mine, q_ref, do_ref, o_ref, lse_ref, k_ref, v_ref,
    dq_ref, dk_ref, dv_ref, k_seq, v_seq, dk_seq, dv_seq,
):
    block_rows = q_ref.shape[0] // 2
    tile_rows = key_tile_rows(k_ref.shape[0])
    to_sequence(table, block_rows, ((k_ref, k_seq), (v_ref, v_seq)))

    def clear(tile, _):
        place = pl.ds(pl.multiple_of(tile * tile_rows, tile_rows), tile_rows)
        zero = jnp.zeros((tile_rows, dk_seq.shape[1]), jnp.float32)
        dk_seq[place, :] = zero
        dv_seq[place, :] = zero
        return 0

    lax.fori_loop(0, k_ref.shape[0] // tile_rows, clear, 0)
    for half in range(2):
        rows = pl.ds(half * block_rows, block_rows)
        queries = head_halves(q_ref[rows, :])
        grads = head_halves(do_ref[rows, :])
        attended = o_ref[rows, :]
        delta = jnp.sum(
            grads.astype(jnp.float32) * jnp.concatenate([attended, attended], 0), -1, keepdims=True
        )
        log_total = lse_ref[0, pl.ds(half * 2 * block_rows, 2 * block_rows), :][:, :1]
        first = mine[half] * block_rows

        def step(tile, total, masked):
            place = pl.ds(pl.multiple_of(tile * tile_rows, tile_rows), tile_rows)
            keys = k_seq[place, :]
            scores = times_transpose(queries, keys)
            if masked:
                scores = jnp.where(
                    allowed_mask(first, block_rows, tile, tile_rows), scores, NEGATIVE
                )
            chances = jnp.exp(scores - log_total)
            dchance = times_transpose(grads, v_seq[place, :])
            dscores = (chances * (dchance - delta)).astype(jnp.bfloat16)
            dk_seq[place, :] += outer_sum(dscores, queries)
            dv_seq[place, :] += outer_sum(chances.astype(jnp.bfloat16), grads)
            return total + matmul(dscores, keys)

        full = (first + 1) // tile_rows
        count = (first + block_rows - 1) // tile_rows + 1
        total = jnp.zeros((2 * block_rows, q_ref.shape[1]), jnp.float32)
        total = lax.fori_loop(0, full, lambda t, c: step(t, c, False), total)
        total = lax.fori_loop(full, count, lambda t, c: step(t, c, True), total)
        dq_ref[rows, :] = join_halves(total).astype(dq_ref.dtype)

    def back(slot, _):
        target = pl.ds(pl.multiple_of(slot * block_rows, block_rows), block_rows)
        source = pl.ds(pl.multiple_of(table[slot] * block_rows, block_rows), block_rows)
        dk_ref[target, :] = dk_seq[source, :].astype(dk_ref.dtype)
        dv_ref[target, :] = dv_seq[source, :].astype(dv_ref.dtype)
        return 0

    lax.fori_loop(0, table.shape[0], back, 0)


LANES = 2 * HD


def wide_spec(length, shift):
    spare = {} if length <= 8192 else {"pipeline_mode": pl.Buffered(1)}
    return pl.BlockSpec((length, LANES), lambda h, *_: (0, h + shift), **spare)


def attention_cost(length, rows, pairs, products):
    area = rows * length // 2
    return pl.CostEstimate(
        flops=products * 2 * area * LANES * 2 * pairs,
        bytes_accessed=8 * length * LANES * pairs,
        transcendentals=2 * area * pairs,
    )


def attend(queries, kv_all, dealt, mine):
    rows, width = queries.shape
    length = kv_all.shape[0]
    pairs = width // LANES
    small = pl.BlockSpec((rows, LANES), lambda h, *_: (0, h))
    return pl.pallas_call(
        forward_kernel,
        out_shape=(
            jax.ShapeDtypeStruct((rows, width), jnp.float32),
            jax.ShapeDtypeStruct((pairs, 2 * rows, LANES), jnp.float32),
        ),
        grid_spec=pltpu.PrefetchScalarGridSpec(
            num_scalar_prefetch=2,
            grid=(pairs,),
            in_specs=[small, wide_spec(length, 0), wide_spec(length, pairs)],
            out_specs=[small, pl.BlockSpec((1, 2 * rows, LANES), lambda h, *_: (h, 0, 0))],
            scratch_shapes=[pltpu.VMEM((length, LANES), jnp.bfloat16)] * 2,
        ),
        compiler_params=pltpu.CompilerParams(vmem_limit_bytes=(32 if length <= 8192 else 56) << 20),
        cost_estimate=attention_cost(length, rows, pairs, 2),
    )(dealt, mine, queries, kv_all, kv_all)


def attend_back(queries, grads, attended, log_total, kv_all, dealt, mine):
    rows, width = queries.shape
    length = kv_all.shape[0]
    pairs = width // LANES
    small = pl.BlockSpec((rows, LANES), lambda h, *_: (0, h))
    wide = jax.ShapeDtypeStruct((length, width), jnp.bfloat16)
    return pl.pallas_call(
        backward_kernel,
        out_shape=(jax.ShapeDtypeStruct((rows, width), jnp.bfloat16), wide, wide),
        grid_spec=pltpu.PrefetchScalarGridSpec(
            num_scalar_prefetch=2,
            grid=(pairs,),
            in_specs=[
                small,
                small,
                small,
                pl.BlockSpec((1, 2 * rows, LANES), lambda h, *_: (h, 0, 0)),
                wide_spec(length, 0),
                wide_spec(length, pairs),
            ],
            out_specs=[small, wide_spec(length, 0), wide_spec(length, 0)],
            scratch_shapes=[pltpu.VMEM((length, LANES), jnp.bfloat16)] * 2
            + [pltpu.VMEM((length, LANES), jnp.float32)] * 2,
        ),
        compiler_params=pltpu.CompilerParams(vmem_limit_bytes=(32 if length <= 8192 else 60) << 20),
        cost_estimate=attention_cost(length, rows, pairs, 5),
    )(dealt, mine, queries, grads, attended, log_total, kv_all, kv_all)


def gather_vectors(vectors):
    sizes = [v.shape[0] for v in vectors]
    both = lax.all_gather(jnp.concatenate(vectors), "shard", axis=0)
    out, at = [], 0
    for size in sizes:
        out.append(both[:, at : at + size].reshape(-1).astype(jnp.float32))
        at += size
    return out


def sum_vectors(vectors):
    halves = lax.axis_size("shard")
    sizes = [v.shape[0] // halves for v in vectors]
    packed = jnp.concatenate([v.reshape(halves, -1) for v in vectors], 1)
    summed = lax.psum(packed, ("ctx", "shard"))
    here = lax.dynamic_index_in_dim(summed, lax.axis_index("shard"), 0, keepdims=False)
    out, at = [], 0
    for size in sizes:
        out.append(here[at : at + size])
        at += size
    return out


def sum_matrix(term):
    share = lax.psum_scatter(term.astype(jnp.bfloat16), "shard", scatter_dimension=0, tiled=True)
    return lax.psum(share, "ctx").astype(jnp.float32)


def body(
    inputs,
    cotangent,
    block_table,
    first_gain,
    first_shift,
    query_weight,
    query_bias,
    keyvalue_weight,
    value_bias,
    out_weight,
    out_bias,
    second_gain,
    second_shift,
    up_weight,
    up_bias,
    down_weight,
    down_bias,
):
    my_index = lax.axis_index("ctx")
    dealt = block_table.reshape(-1)
    mine = lax.dynamic_index_in_dim(block_table, my_index, 0, keepdims=False)
    gain_one, shift_one, b_query, b_value, b_out, gain_two, shift_two, b_up, b_down = gather_vectors(
        [
            first_gain,
            first_shift,
            query_bias,
            value_bias,
            out_bias,
            second_gain,
            second_shift,
            up_bias,
            down_bias,
        ]
    )
    w_keyvalue = lax.all_gather(keyvalue_weight, "shard", axis=0, tiled=True)
    w_query = lax.all_gather(query_weight, "shard", axis=0, tiled=True)
    w_down = lax.all_gather(down_weight, "shard", axis=0, tiled=True)
    w_out = lax.all_gather(out_weight, "shard", axis=0, tiled=True)
    w_up = lax.all_gather(up_weight, "shard", axis=0, tiled=True)
    kv_shift = jnp.concatenate([jnp.zeros_like(b_value), b_value])
    hidden = inputs[0].astype(jnp.float32)
    normed = normalize(hidden, gain_one, shift_one).astype(jnp.bfloat16)
    kv_local = (matmul(normed, w_keyvalue) + kv_shift).astype(jnp.bfloat16)
    kv_all = lax.all_gather(kv_local, "ctx", axis=0, tiled=True)
    queries = ((matmul(normed, w_query) + b_query) * 0.125).astype(jnp.bfloat16)
    down_grad_in = cotangent[0]
    upstream = down_grad_in.astype(jnp.float32)
    dactive = times_transpose(down_grad_in, w_down)
    attended, log_total = attend(queries, kv_all, dealt, mine)
    attended_low = attended.astype(jnp.bfloat16)
    middle = hidden + matmul(attended_low, w_out) + b_out
    second = normalize(middle, gain_two, shift_two).astype(jnp.bfloat16)
    pre_act = matmul(second, w_up) + b_up
    active = gelu_tanh(pre_act).astype(jnp.bfloat16)
    down_grad = sum_matrix(outer_sum(active, down_grad_in))
    _, gelu_pull = jax.vjp(gelu_tanh, pre_act)
    dpre = gelu_pull(dactive)[0].astype(jnp.bfloat16)
    up_grad = sum_matrix(outer_sum(second, dpre))
    result = middle + matmul(active, w_down) + b_down
    dsecond = times_transpose(dpre, w_up)
    _, norm_pull_two = jax.vjp(normalize, middle, gain_two, shift_two)
    dmiddle_part, dgain_two, dshift_two = norm_pull_two(dsecond)
    dmiddle = upstream + dmiddle_part
    dbranch = dmiddle.astype(jnp.bfloat16)
    dattended = times_transpose(dbranch, w_out).astype(jnp.bfloat16)
    dquery, dkey_all, dvalue_all = attend_back(
        queries, dattended, attended, log_total, kv_all, dealt, mine
    )
    out_grad = sum_matrix(outer_sum(attended_low, dbranch))
    dkey = lax.psum_scatter(dkey_all, "ctx", scatter_dimension=0, tiled=True)
    dvalue = lax.psum_scatter(dvalue_all, "ctx", scatter_dimension=0, tiled=True)
    query_grad = sum_matrix(outer_sum(normed, dquery) * 0.125)
    kv_grad_low = jnp.concatenate([dkey, dvalue], 1)
    keyvalue_grad = sum_matrix(outer_sum(normed, kv_grad_low))
    dnormed = times_transpose(dquery, w_query) * 0.125 + times_transpose(kv_grad_low, w_keyvalue)
    _, norm_pull_one = jax.vjp(normalize, hidden, gain_one, shift_one)
    dhidden_part, dgain_one, dshift_one = norm_pull_one(dnormed)
    input_grad = (dmiddle + dhidden_part).astype(jnp.bfloat16)
    (
        gain_one_grad,
        shift_one_grad,
        query_bias_grad,
        value_bias_grad,
        out_bias_grad,
        gain_two_grad,
        shift_two_grad,
        up_bias_grad,
        down_bias_grad,
    ) = sum_vectors(
        [
            dgain_one,
            dshift_one,
            jnp.sum(dquery.astype(jnp.float32), 0) * 0.125,
            jnp.sum(dvalue.astype(jnp.float32), 0),
            jnp.sum(dbranch.astype(jnp.float32), 0),
            dgain_two,
            dshift_two,
            jnp.sum(dpre.astype(jnp.float32), 0),
            jnp.sum(upstream, 0),
        ]
    )
    return (
        result.astype(jnp.bfloat16)[None],
        input_grad[None],
        gain_one_grad,
        shift_one_grad,
        query_grad,
        query_bias_grad,
        keyvalue_grad,
        value_bias_grad,
        out_grad,
        out_bias_grad,
        gain_two_grad,
        shift_two_grad,
        up_grad,
        up_bias_grad,
        down_grad,
        down_bias_grad,
    )


def solution(mesh):
    in_specs = (
        P("shard", "ctx", None),
        P("shard", "ctx", None),
        P(),
        P("shard"),
        P("shard"),
        P("shard", None),
        P("shard"),
        P("shard", None),
        P("shard"),
        P("shard", None),
        P("shard"),
        P("shard"),
        P("shard"),
        P("shard", None),
        P("shard"),
        P("shard", None),
        P("shard"),
    )
    out_specs = (
        P("shard", "ctx", None),
        P("shard", "ctx", None),
        P("shard"),
        P("shard"),
        P("shard", None),
        P("shard"),
        P("shard", None),
        P("shard"),
        P("shard", None),
        P("shard"),
        P("shard"),
        P("shard"),
        P("shard", None),
        P("shard"),
        P("shard", None),
        P("shard"),
    )
    return jax.shard_map(body, mesh=mesh, in_specs=in_specs, out_specs=out_specs, check_vma=False)
```

time: 3140 us -> 985 us (0.31)
  blocking collectives: 1180 us -> 46.5 us
  local copies, waits for them, and re-layouts: 772 us -> 27.8 us
  other arithmetic: 304 us -> 21.3 us
  matrix products: 243 us -> 57.5 us
  waiting for transfers between devices: 581 us -> 717 us
  Pallas kernels: 0 us -> 98.3 us
    psum x1, blocking collectives: 1160 us -> 44.5 us  [sum_vectors(): summed = lax.psum(packed, ('ctx', 'shard'))]
    gather x9 -> x0, local copies, waits for them, and re-layouts: 191 us -> none  [fetch_tile(): chosen = jnp.take(blocks, picks, axis=0)]
    reshape x13 -> x9, local copies, waits for them, and re-layouts: 190 us -> 0.17 us  [the longest x1 0.09 us: body(): dealt = block_table.reshape(-1)]
    dot_general x21 -> x0, matrix products: 188 us -> none  [the longest x6 59.1 us: scores_against(): jnp.einsum('qhd,khd->hqk', query_rows, key_tile[:, 0], preferred_element_...]
    select_n x9 -> x0, local copies, waits for them, and re-layouts: 188 us -> none  [fetch_tile(): chosen = jnp.take(blocks, picks, axis=0)]
    psum x0 -> x1, waiting for transfers between devices: none -> 181 us  [sum_matrix(): return lax.psum(share, 'ctx').astype(jnp.float32)]
    another operation x17 -> x0, local copies, waits for them, and re-layouts: 147 us -> none  [the longest x9 147 us: grad_step(): jnp.stack([key_grad, value_grad], 1)]
    pallas_call x0 -> x2, Pallas kernels: none -> 98.3 us  [the longest x1 60.8 us: attend_back(): pl.pallas_call(backward_kernel, out_shape=(jax.ShapeDtypeStruct((rows, wi...]
  transfers between devices with their start and end apart: 12 -> 14, of which waited for: 7 -> 11; matrix products, arithmetic and copies ran while one was open for 19% -> 7% of each run, Pallas kernels for 0% -> 4%
where the time goes in v1:
time: 985 us; the launch traced here: 984 us
  waiting for transfers between devices  717 us (73%)
  Pallas kernels  98.3 us (10%)
  matrix products  57.5 us (6%)
  blocking collectives  46.5 us (5%)
  local copies, waits for them, and re-layouts  27.8 us (3%)
  other arithmetic  21.3 us (2%)
  between operations  14.5 us (1%)
    psum x1, waiting for transfers between devices, sum_matrix(): return lax.psum(share, 'ctx').astype(jnp.float32)  181 us
    all_gather x1, waiting for transfers between devices, body(): kv_all = lax.all_gather(kv_local, 'ctx', axis=0, tiled=True)  170 us
    reduce_scatter x1, waiting for transfers between devices, body(): lax.psum_scatter(dvalue_all, 'ctx', scatter_dimension=0, tiled=True)  154 us
    reduce_scatter x1, waiting for transfers between devices, body(): dkey = lax.psum_scatter(dkey_all, 'ctx', scatter_dimension=0, tiled=True)  137 us
    reduce_scatter x5, waiting for transfers between devices, sum_matrix(): lax.psum_scatter(term.astype(jnp.bfloat16), 'shard', scatter_dimension=0,...  66.1 us
    pallas_call x1, Pallas kernels, attend_back(): pl.pallas_call(backward_kernel, out_shape=(jax.ShapeDtypeStruct((rows, wi...  60.8 us
    psum x1, blocking collectives, sum_vectors(): summed = lax.psum(packed, ('ctx', 'shard'))  44.5 us
    pallas_call x1, Pallas kernels, attend(): pl.pallas_call(forward_kernel, out_shape=(jax.ShapeDtypeStruct((rows, wid...  37.5 us
  transfers between devices with their start and end apart: 14, of which 11 were waited for; matrix products, arithmetic and copies ran while one was open for 7% of the time, Pallas kernels for 4%

profile of v1, /device:TPU:0, one launch (start us, length us, event | category | flops | bytes accessed | tf_op | source)
XLA Modules:
  0.0 983.6 jit_solution(10180266104663888670)
XLA Ops:
  23.3 3.7 fusion.7
  31.7 3.5 all-gather.9.cloned.1.call-done
  37.1 169.6 %all-gather.13.cloned.1.call-done.k_ref.v_ref = bf16[4608,1536]{1,0:T(8,128)(2,1)} async-done(((bf16[288,1536]{1,0:T(8,128)(2,1)}), bf16[4608,1536]{1,0:T(8,128)(2,1)}) %all-gather.13.cloned.1.call-update) | async-done | bytes 14155792 | tf_op jit(solution)/shard_map/all_gather | solution.py:322
  206.7 5.0 copy-done
  211.7 37.5 %shard_map.288 = (f32[288,768]{1,0:T(8,128)S(1)}, f32[6,576,128]{2,1,0:T(8,128)S(1)}) custom-call(s32[32]{0:T(128)S(1)} %reshape.205.table, s32[2]{0:T(128)S(1)} %dynamic-slice_reduce_fusion.9.mine, bf16[288,768]{1,0:T(8,128)(2,1)S(1)} %fusion.12.q_ref, bf16[4608,1536]{1,0:T(8,128)(2,1)S(1)} %copy-done, bf16[4608,1536]{1,0:T(8,128)(2,1)S(1)} %copy-done), custom_call_target="tpu_custom_call" | custom-call | flops 4076863488 | bytes 28311552 | tf_op jit(solution)/shard_map/pallas_call | solution.py:203
  254.6 6.1 convolution_add_fusion
  260.7 7.8 convert_reduce_fusion
  268.6 4.2 multiply_reduce_fusion
  276.2 60.8 %shard_map.289 = (bf16[288,768]{1,0:T(8,128)(2,1)S(1)}, bf16[4608,768]{1,0:T(8,128)(2,1)S(1)}, bf16[4608,768]{1,0:T(8,128)(2,1)S(1)}) custom-call(s32[32]{0:T(128)S(1)} %reshape.205.table, s32[2]{0:T(128)S(1)} %dynamic-slice_reduce_fusion.9.mine, bf16[288,768]{1,0:T(8,128)(2,1)S(1)} %fusion.12.q_ref, bf16[288,768]{1,0:T(8,128)(2,1)S(1)} %convolution_convert_fusion.4.do_ref, ...), custom_call_target="tpu_custom_call" | custom-call | flops 10192158720 | bytes 28311552 | tf_op jit(solution)/shard_map/pallas_call | solution.py:227
  337.0 2.9 copy-done.1
  347.8 6.8 convolution_convert_fusion.1
  355.6 7.4 convolution_convert_fusion
  363.4 136.9 %reduce-scatter.8.cloned.1.call-done = bf16[288,768]{1,0:T(8,128)(2,1)} async-done(((bf16[4608,768]{1,0:T(8,128)(2,1)}), bf16[288,768]{1,0:T(8,128)(2,1)}) %reduce-scatter.8.cloned.1.call-update) | async-done | bytes 442384 | tf_op jit(solution)/shard_map/reduce_scatter | solution.py:348
  501.3 154.3 %reduce-scatter.10.cloned.1.call-done = bf16[288,768]{1,0:T(8,128)(2,1)} async-done(((bf16[4608,768]{1,0:T(8,128)(2,1)}), bf16[288,768]{1,0:T(8,128)(2,1)}) %reduce-scatter.10.cloned.1.call-update) | async-done | bytes 442384 | tf_op jit(solution)/shard_map/reduce_scatter | solution.py:349
  656.7 3.0 convolution_convert_fusion.2
  659.7 6.2 reduce-scatter.12.cloned.1.call-done
  665.9 12.6 %reduce-scatter.16.cloned.1.call-done = bf16[384,768]{1,0:T(8,128)(2,1)} async-done(((bf16[768,768]{1,0:T(8,128)(2,1)}), bf16[384,768]{1,0:T(8,128)(2,1)}) %reduce-scatter.16.cloned.1.call-update) | async-done | bytes 589840 | tf_op jit(solution)/shard_map/reduce_scatter | solution.py:274
  678.6 16.7 %reduce-scatter.18.cloned.1.call-done = bf16[384,3072]{1,0:T(8,128)(2,1)} async-done(((bf16[768,3072]{1,0:T(8,128)(2,1)}), bf16[384,3072]{1,0:T(8,128)(2,1)}) %reduce-scatter.18.cloned.1.call-update) | async-done | bytes 2359312 | tf_op jit(solution)/shard_map/reduce_scatter | solution.py:274
  695.3 16.6 %reduce-scatter.20.cloned.1.call-done = bf16[1536,768]{1,0:T(8,128)(2,1)} async-done(((bf16[3072,768]{1,0:T(8,128)(2,1)}), bf16[1536,768]{1,0:T(8,128)(2,1)}) %reduce-scatter.20.cloned.1.call-update) | async-done | bytes 2359312 | tf_op jit(solution)/shard_map/reduce_scatter | solution.py:274
  711.9 13.9 %reduce-scatter.14.cloned.1.call-done = bf16[384,1536]{1,0:T(8,128)(2,1)} async-done(((bf16[768,1536]{1,0:T(8,128)(2,1)}), bf16[384,1536]{1,0:T(8,128)(2,1)}) %reduce-scatter.14.cloned.1.call-update) | async-done | bytes 1179664 | tf_op jit(solution)/shard_map/reduce_scatter | solution.py:274
  728.5 6.7 fusion.13
  738.3 44.5 %psum.42 = f32[2,4608]{1,0:T(2,128)S(1)} all-reduce(f32[2,4608]{1,0:T(2,128)S(1)} %constant_dynamic-update-slice_fusion.2), channel_id=1, replica_groups=mesh['ctx'=16,'shard'=2] {'ctx','shard'}, use_global_device_ids=true, to_apply=%region_19.20 | all-reduce | flops 9216 | bytes 73728 | tf_op jit(solution)/shard_map/psum | solution.py:264
  784.2 181.1 %all-reduce.4.cloned.1.call-done = (bf16[384,768]{1,0:T(8,128)(2,1)}, bf16[384,1536]{1,0:T(8,128)(2,1)}, bf16[384,768]{1,0:T(8,128)(2,1)}, bf16[384,3072]{1,0:T(8,128)(2,1)}, bf16[1536,768]{1,0:T(8,128)(2,1)}) async-done(((bf16[384,768]{1,0:T(8,128)(2,1)}, bf16[384,1536]{1,0:T(8,128)(2,1)}, bf16[384,768]{1,0:T(8,128)(2,1)}, bf16[384,3072]{1,0:T(8,128)(2,1)}, bf16[1536,768]{1,0:T(8,128)(2,1)}), ...) | async-done | bytes 7077904 | tf_op jit(solution)/shard_map/psum | solution.py:275
  967.6 3.0 convert_element_type.206
  (201 shorter events, 58.3 us)
Async XLA Ops:
  7.2 16.1 %all-gather.11.cloned.1.call-start = ((), (), s32[]{:S(2)}) async-start(), calls=%async_computation.8 | async-start | bytes 3538944 | tf_op jit(solution)/shard_map/all_gather | solution.py:313
  7.9 27.3 %all-gather.9.cloned.1.call-start = ((), (), s32[]{:S(2)}) async-start(), calls=%async_computation.7 | async-start | bytes 1769472 | tf_op jit(solution)/shard_map/all_gather | solution.py:314
  8.7 198.0 %all-gather.13.cloned.1.call-start = ((), (), s32[]{:S(2)}) async-start(), calls=%async_computation.9 | async-start | bytes 15040512 | tf_op jit(solution)/shard_map/all_gather | solution.py:322
  19.0 16.2 %copy-start.37 = (f32[768]{0:T(1024)}, f32[768]{0:T(1024)S(1)}, u32[]{:S(2)}) copy-start(f32[768]{0:T(1024)S(1)} %reshape.215) | copy-start | bytes 9220
  21.6 13.6 %copy-start.23 = (f32[288]{0:T(512)}, f32[288]{0:T(512)S(1)}, u32[]{:S(2)}) copy-start(f32[288]{0:T(512)S(1)} %fusion.35) | copy-start | bytes 3460
  26.9 8.3 copy-start.3
  27.0 222.3 %all-gather.15.cloned.1.call-start = ((), (), s32[]{:S(2)}) async-start(), calls=%async_computation.10 | async-start | bytes 1769472 | tf_op jit(solution)/shard_map/all_gather | solution.py:316
  27.5 227.1 %all-gather.17.cloned.1.call-start = ((), (), s32[]{:S(2)}) async-start(), calls=%async_computation.11 | async-start | bytes 7077888 | tf_op jit(solution)/shard_map/all_gather | solution.py:317
  28.1 232.6 %all-gather.19.cloned.1.call-start = ((), (), s32[]{:S(2)}) async-start(), calls=%async_computation.12 | async-start | bytes 7077888 | tf_op jit(solution)/shard_map/all_gather | solution.py:315
  28.7 471.5 %reduce-scatter.8.cloned.1.call-start = ((), (), s32[]{:S(2)}) async-start(), calls=%async_computation.13 | async-start | bytes 7520256 | tf_op jit(solution)/shard_map/reduce_scatter | solution.py:348
  260.7 7.9 copy-start.26
  260.7 7.9 copy-start.31
  260.7 7.9 copy-start.35
  260.7 7.9 copy-start.43
  342.7 312.9 %reduce-scatter.10.cloned.1.call-start = ((), (), s32[]{:S(2)}) async-start(), calls=%async_computation.14 | async-start | bytes 7520256 | tf_op jit(solution)/shard_map/reduce_scatter | solution.py:349
  343.5 322.4 %reduce-scatter.12.cloned.1.call-start = ((), (), s32[]{:S(2)}) async-start(), calls=%async_computation.15 | async-start | bytes 1769472 | tf_op jit(solution)/shard_map/reduce_scatter | solution.py:274
  345.8 332.7 %reduce-scatter.16.cloned.1.call-start = ((), (), s32[]{:S(2)}) async-start(), calls=%async_computation.17 | async-start | bytes 1769472 | tf_op jit(solution)/shard_map/reduce_scatter | solution.py:274
  347.7 347.5 %reduce-scatter.18.cloned.1.call-start = ((), (), s32[]{:S(2)}) async-start(), calls=%async_computation.18 | async-start | bytes 7077888 | tf_op jit(solution)/shard_map/reduce_scatter | solution.py:274
  354.6 357.3 %reduce-scatter.20.cloned.1.call-start = ((), (), s32[]{:S(2)}) async-start(), calls=%async_computation.19 | async-start | bytes 7077888 | tf_op jit(solution)/shard_map/reduce_scatter | solution.py:274
  363.1 362.7 %reduce-scatter.14.cloned.1.call-start = ((), (), s32[]{:S(2)}) async-start(), calls=%async_computation.16 | async-start | bytes 3538944 | tf_op jit(solution)/shard_map/reduce_scatter | solution.py:274
  659.7 305.7 %all-reduce.4.cloned.1.call-start = ((), (), s32[]{:S(2)}) async-start(), calls=%async_computation.20 | async-start | bytes 14155776 | tf_op jit(solution)/shard_map/psum | solution.py:275
  728.5 6.7 copy-start.18
  728.5 6.7 copy-start.44
  965.3 6.4 copy-start.8
  (36 other events, 90.5 us)
Sparse Core Ops, SparseCore 0:
  9.6 13.6 all-gather.10
  24.8 10.3 all-gather.8
  38.6 168.0 all-gather.12
  208.1 7.4 all-gather.14
  216.9 15.6 all-gather.16
  234.0 15.6 all-gather.18
  342.8 157.3 reduce-scatter.7
  505.6 149.9 reduce-scatter.9
  658.4 7.4 reduce-scatter.11
  668.7 9.8 reduce-scatter.15
  681.4 13.7 reduce-scatter.17
  698.1 13.7 reduce-scatter.19
  714.7 11.0 reduce-scatter.13
  733.2 232.0 all-reduce.3

commit v2 on v1

v2 whole, which is shorter than its diff:
```python
import jax
import jax.numpy as jnp
from jax import lax
from jax.experimental import pallas as pl
from jax.experimental.pallas import tpu as pltpu
from jax.sharding import PartitionSpec as P

HD = 64


EPSILON = 1e-05
NEGATIVE = -1e30


def normalize(values, gain, shift):
    centre = values - jnp.mean(values, -1, keepdims=True)
    spread = jnp.mean(centre * centre, -1, keepdims=True)
    return centre * lax.rsqrt(spread + EPSILON) * gain + shift


def gelu_tanh(values):
    return jax.nn.gelu(values, approximate=True)


def matmul(left, right):
    return jnp.dot(left, right, preferred_element_type=jnp.float32)


def outer_sum(left, right):
    return lax.dot_general(
        left, right, (((0,), (0,)), ((), ())), preferred_element_type=jnp.float32
    )


def times_transpose(left, right):
    return lax.dot_general(
        left, right, (((1,), (1,)), ((), ())), preferred_element_type=jnp.float32
    )


def key_tile_rows(length):
    for rows in (512, 384, 256, 128):
        if length % rows == 0:
            return rows
    return length


def stack_heads(rows):
    block_rows, lanes = rows.shape
    head = lax.broadcasted_iota(jnp.int32, (block_rows, lanes), 1) // HD
    parts = [
        rows * (head == h).astype(jnp.float32).astype(rows.dtype) for h in range(lanes // HD)
    ]
    return jnp.concatenate(parts, 0)


def join_heads(stacked):
    lanes = stacked.shape[1]
    block_rows = stacked.shape[0] // (lanes // HD)
    head = lax.broadcasted_iota(jnp.int32, (block_rows, lanes), 1) // HD
    result = stacked[:block_rows]
    for h in range(1, lanes // HD):
        result = jnp.where(head == h, stacked[h * block_rows : (h + 1) * block_rows], result)
    return result


def to_sequence(table, block_rows, pairs):
    def move(slot, _):
        source = pl.ds(pl.multiple_of(slot * block_rows, block_rows), block_rows)
        target = pl.ds(pl.multiple_of(table[slot] * block_rows, block_rows), block_rows)
        for dealt, ordered in pairs:
            ordered[target, :] = dealt[source, :]
        return 0

    lax.fori_loop(0, table.shape[0], move, 0)


def allowed_mask(first, block_rows, heads, tile, tile_rows):
    shape = (block_rows, tile_rows)
    row = lax.broadcasted_iota(jnp.int32, shape, 0)
    col = lax.broadcasted_iota(jnp.int32, shape, 1)
    return jnp.concatenate([row - col] * heads, 0) >= tile * tile_rows - first


def forward_kernel(table, mine, q_ref, k_ref, v_ref, o_ref, lse_ref, k_seq, v_seq):
    block_rows, lanes = q_ref.shape
    heads = lanes // HD
    rows = heads * block_rows
    tile_rows = key_tile_rows(k_ref.shape[0])
    which = pl.program_id(0)

    @pl.when(which == 0)
    def _():
        to_sequence(table, block_rows, ((k_ref, k_seq), (v_ref, v_seq)))

    queries = stack_heads(q_ref[...])
    first = mine[which] * block_rows

    def step(tile, carry, masked):
        running, denominator, total = carry
        place = pl.ds(pl.multiple_of(tile * tile_rows, tile_rows), tile_rows)
        scores = times_transpose(queries, k_seq[place, :])
        if masked:
            allowed = allowed_mask(first, block_rows, heads, tile, tile_rows)
            scores = jnp.where(allowed, scores, NEGATIVE)
        new_running = jnp.maximum(running, jnp.max(scores, -1, keepdims=True))
        decay = jnp.exp(running - new_running)
        chances = jnp.exp(scores - new_running)
        denominator = denominator * decay + jnp.sum(chances, -1, keepdims=True)
        total = total * decay + matmul(chances.astype(jnp.bfloat16), v_seq[place, :])
        return new_running, denominator, total

    start = (
        jnp.full((rows, 1), NEGATIVE, jnp.float32),
        jnp.zeros((rows, 1), jnp.float32),
        jnp.zeros((rows, lanes), jnp.float32),
    )
    full = (first + 1) // tile_rows
    count = (first + block_rows - 1) // tile_rows + 1
    carry = lax.fori_loop(0, full, lambda t, c: step(t, c, False), start)
    running, denominator, total = lax.fori_loop(full, count, lambda t, c: step(t, c, True), carry)
    o_ref[...] = join_heads(total / denominator)
    lse_ref[0] = jnp.broadcast_to(running + jnp.log(denominator), (rows, lse_ref.shape[2]))


def backward_kernel(
    table, mine, q_ref, do_ref, o_ref, lse_ref, k_ref, v_ref,
    dq_ref, dk_ref, dv_ref, k_seq, v_seq, dk_seq, dv_seq,
):
    block_rows, lanes = q_ref.shape
    heads = lanes // HD
    rows = heads * block_rows
    tile_rows = key_tile_rows(k_ref.shape[0])
    which = pl.program_id(0)

    @pl.when(which == 0)
    def _():
        to_sequence(table, block_rows, ((k_ref, k_seq), (v_ref, v_seq)))

        def clear(tile, _):
            place = pl.ds(pl.multiple_of(tile * tile_rows, tile_rows), tile_rows)
            zero = jnp.zeros((tile_rows, lanes), jnp.float32)
            dk_seq[place, :] = zero
            dv_seq[place, :] = zero
            return 0

        lax.fori_loop(0, k_ref.shape[0] // tile_rows, clear, 0)

    queries = stack_heads(q_ref[...])
    grads = stack_heads(do_ref[...])
    delta = jnp.sum(
        grads.astype(jnp.float32) * jnp.concatenate([o_ref[...]] * heads, 0), -1, keepdims=True
    )
    log_total = lse_ref[0][:, :1]
    first = mine[which] * block_rows

    def step(tile, total, masked):
        place = pl.ds(pl.multiple_of(tile * tile_rows, tile_rows), tile_rows)
        keys = k_seq[place, :]
        scores = times_transpose(queries, keys)
        if masked:
            allowed = allowed_mask(first, block_rows, heads, tile, tile_rows)
            scores = jnp.where(allowed, scores, NEGATIVE)
        chances = jnp.exp(scores - log_total)
        dchance = times_transpose(grads, v_seq[place, :])
        dscores = (chances * (dchance - delta)).astype(jnp.bfloat16)
        dk_seq[place, :] += outer_sum(dscores, queries)
        dv_seq[place, :] += outer_sum(chances.astype(jnp.bfloat16), grads)
        return total + matmul(dscores, keys)

    full = (first + 1) // tile_rows
    count = (first + block_rows - 1) // tile_rows + 1
    total = jnp.zeros((rows, lanes), jnp.float32)
    total = lax.fori_loop(0, full, lambda t, c: step(t, c, False), total)
    total = lax.fori_loop(full, count, lambda t, c: step(t, c, True), total)
    dq_ref[...] = join_heads(total).astype(dq_ref.dtype)

    @pl.when(which == pl.num_programs(0) - 1)
    def _():
        def back(slot, _):
            target = pl.ds(pl.multiple_of(slot * block_rows, block_rows), block_rows)
            source = pl.ds(pl.multiple_of(table[slot] * block_rows, block_rows), block_rows)
            dk_ref[target, :] = dk_seq[source, :].astype(dk_ref.dtype)
            dv_ref[target, :] = dv_seq[source, :].astype(dv_ref.dtype)
            return 0

        lax.fori_loop(0, table.shape[0], back, 0)


STAT_LANES = 128


def attention_cost(length, rows, lanes, products):
    area = rows * length // 2
    return pl.CostEstimate(
        flops=products * 2 * area * lanes,
        bytes_accessed=8 * length * lanes,
        transcendentals=2 * area * lanes // HD,
    )


def attention_call(kernel, operands, dealt, mine, keys, values):
    back = len(operands) > 1
    rows, lanes = operands[0].shape
    length = keys.shape[0]
    blocks = mine.shape[0]
    block_rows = rows // blocks
    stacked = block_rows * lanes // HD
    small = pl.BlockSpec((block_rows, lanes), lambda b, *_: (b, 0))
    stats = pl.BlockSpec((1, stacked, STAT_LANES), lambda b, *_: (b, 0, 0))
    wide = pl.BlockSpec((length, lanes), lambda b, *_: (0, 0), pipeline_mode=pl.Buffered(1))
    if back:
        in_specs, out_specs = [small, small, small, stats, wide, wide], [small, wide, wide]
        grad = jax.ShapeDtypeStruct((length, lanes), jnp.bfloat16)
        out_shape = (jax.ShapeDtypeStruct((rows, lanes), jnp.bfloat16), grad, grad)
    else:
        in_specs, out_specs = [small, wide, wide], [small, stats]
        out_shape = (
            jax.ShapeDtypeStruct((rows, lanes), jnp.float32),
            jax.ShapeDtypeStruct((blocks, stacked, STAT_LANES), jnp.float32),
        )
    scratch = [pltpu.VMEM((length, lanes), jnp.bfloat16)] * 2
    if back:
        scratch = scratch + [pltpu.VMEM((length, lanes), jnp.float32)] * 2
    return pl.pallas_call(
        kernel,
        out_shape=out_shape,
        grid_spec=pltpu.PrefetchScalarGridSpec(
            num_scalar_prefetch=2,
            grid=(blocks,),
            in_specs=in_specs,
            out_specs=out_specs,
            scratch_shapes=scratch,
        ),
        compiler_params=pltpu.CompilerParams(vmem_limit_bytes=(44 if length <= 8192 else 58) << 20),
        cost_estimate=attention_cost(length, rows, lanes, 5 if back else 2),
    )(dealt, mine, *operands, keys, values)


def head_parts(length, lanes):
    width = lanes if length <= 8192 else HD
    return [slice(at, at + width) for at in range(0, lanes, width)]


def attend(queries, keys, values, dealt, mine):
    results = [
        attention_call(forward_kernel, (queries[:, p],), dealt, mine, keys[:, p], values[:, p])
        for p in head_parts(keys.shape[0], keys.shape[1])
    ]
    return jnp.concatenate([r[0] for r in results], 1), [r[1] for r in results]


def attend_back(queries, grads, attended, stats, keys, values, dealt, mine):
    results = []
    for p, stat in zip(head_parts(keys.shape[0], keys.shape[1]), stats):
        operands = (queries[:, p], grads[:, p], attended[:, p], stat)
        results.append(
            attention_call(backward_kernel, operands, dealt, mine, keys[:, p], values[:, p])
        )
    return [jnp.concatenate([r[i] for r in results], 1) for i in range(3)]


HEAD_GROUPS = 4


def near_groups():
    count = lax.axis_size("ctx")
    return [list(range(at, at + HEAD_GROUPS)) for at in range(0, count, HEAD_GROUPS)]


def far_groups():
    count = lax.axis_size("ctx")
    return [list(range(at, count, HEAD_GROUPS)) for at in range(HEAD_GROUPS)]


def to_heads(arrays):
    rows = arrays[0].shape[0]
    parts = [a.reshape(rows, HEAD_GROUPS, -1).transpose(1, 0, 2) for a in arrays]
    packed = parts[0] if len(parts) == 1 else jnp.concatenate(parts, 2)
    moved = lax.all_to_all(packed, "ctx", 0, 0, axis_index_groups=near_groups(), tiled=True)
    return moved.reshape(HEAD_GROUPS * rows, -1)


def to_tokens(packed, count):
    rows = packed.shape[0] // HEAD_GROUPS
    packed = packed.reshape(HEAD_GROUPS, rows, -1)
    moved = lax.all_to_all(packed, "ctx", 0, 0, axis_index_groups=near_groups(), tiled=True)
    moved = moved.reshape(HEAD_GROUPS, rows, count, -1).transpose(2, 1, 0, 3)
    return moved.reshape(count, rows, -1)


def gather_vectors(vectors):
    sizes = [v.shape[0] for v in vectors]
    both = lax.all_gather(jnp.concatenate(vectors), "shard", axis=0)
    out, at = [], 0
    for size in sizes:
        out.append(both[:, at : at + size].reshape(-1).astype(jnp.float32))
        at += size
    return out


def sum_vectors(vectors):
    halves = lax.axis_size("shard")
    sizes = [v.shape[0] // halves for v in vectors]
    packed = jnp.concatenate([v.reshape(halves, -1) for v in vectors], 1)
    summed = lax.psum(packed, ("ctx", "shard"))
    here = lax.dynamic_index_in_dim(summed, lax.axis_index("shard"), 0, keepdims=False)
    out, at = [], 0
    for size in sizes:
        out.append(here[at : at + size])
        at += size
    return out


def share_of(term):
    return lax.psum_scatter(term.astype(jnp.bfloat16), "shard", scatter_dimension=0, tiled=True)


def body(
    inputs,
    cotangent,
    block_table,
    first_gain,
    first_shift,
    query_weight,
    query_bias,
    keyvalue_weight,
    value_bias,
    out_weight,
    out_bias,
    second_gain,
    second_shift,
    up_weight,
    up_bias,
    down_weight,
    down_bias,
):
    my_index = lax.axis_index("ctx")
    dealt = block_table.reshape(-1)
    first_near = my_index // HEAD_GROUPS * HEAD_GROUPS
    mine = lax.dynamic_slice_in_dim(block_table, first_near, HEAD_GROUPS, 0).reshape(-1)
    model_width = inputs.shape[2]
    lanes = model_width // HEAD_GROUPS
    gain_one, shift_one, b_query, b_value, b_out, gain_two, shift_two, b_up, b_down = gather_vectors(
        [
            first_gain,
            first_shift,
            query_bias,
            value_bias,
            out_bias,
            second_gain,
            second_shift,
            up_bias,
            down_bias,
        ]
    )
    w_keyvalue = lax.all_gather(keyvalue_weight, "shard", axis=0, tiled=True)
    w_query = lax.all_gather(query_weight, "shard", axis=0, tiled=True)
    w_down = lax.all_gather(down_weight, "shard", axis=0, tiled=True)
    w_out = lax.all_gather(out_weight, "shard", axis=0, tiled=True)
    w_up = lax.all_gather(up_weight, "shard", axis=0, tiled=True)
    kv_shift = jnp.concatenate([jnp.zeros_like(b_value), b_value])
    hidden = inputs[0].astype(jnp.float32)
    normed = normalize(hidden, gain_one, shift_one).astype(jnp.bfloat16)
    kv_local = (matmul(normed, w_keyvalue) + kv_shift).astype(jnp.bfloat16)
    queries = ((matmul(normed, w_query) + b_query) * 0.125).astype(jnp.bfloat16)
    down_grad_in = cotangent[0]
    upstream = down_grad_in.astype(jnp.float32)
    dactive = times_transpose(down_grad_in, w_down)
    near = to_heads([queries, kv_local[:, :model_width], kv_local[:, model_width:]])
    near_queries = near[:, :lanes]
    kv_all = lax.all_gather(
        near[:, lanes:], "ctx", axis=0, axis_index_groups=far_groups(), tiled=True
    )
    near_keys, near_values = kv_all[:, :lanes], kv_all[:, lanes:]
    attended, stats = attend(near_queries, near_keys, near_values, dealt, mine)
    attended_low = to_tokens(attended.astype(jnp.bfloat16), 1)[0]
    middle = hidden + matmul(attended_low, w_out) + b_out
    second = normalize(middle, gain_two, shift_two).astype(jnp.bfloat16)
    pre_act = matmul(second, w_up) + b_up
    active = gelu_tanh(pre_act).astype(jnp.bfloat16)
    down_share = share_of(outer_sum(active, down_grad_in))
    _, gelu_pull = jax.vjp(gelu_tanh, pre_act)
    dpre = gelu_pull(dactive)[0].astype(jnp.bfloat16)
    up_share = share_of(outer_sum(second, dpre))
    result = middle + matmul(active, w_down) + b_down
    dsecond = times_transpose(dpre, w_up)
    _, norm_pull_two = jax.vjp(normalize, middle, gain_two, shift_two)
    dmiddle_part, dgain_two, dshift_two = norm_pull_two(dsecond)
    dmiddle = upstream + dmiddle_part
    dbranch = dmiddle.astype(jnp.bfloat16)
    dattended = times_transpose(dbranch, w_out).astype(jnp.bfloat16)
    out_share = share_of(outer_sum(attended_low, dbranch))
    early = lax.psum((down_share, up_share, out_share), "ctx")
    near_dq, near_dk, near_dv = attend_back(
        near_queries, to_heads([dattended]), attended, stats, near_keys, near_values, dealt, mine
    )
    near_dkv = lax.psum_scatter(
        jnp.concatenate([near_dk, near_dv], 1),
        "ctx",
        scatter_dimension=0,
        axis_index_groups=far_groups(),
        tiled=True,
    )
    dquery, dkey, dvalue = to_tokens(jnp.concatenate([near_dq, near_dkv], 1), 3)
    kv_grad_low = jnp.concatenate([dkey, dvalue], 1)
    late_shares = (
        share_of(outer_sum(normed, dquery) * 0.125),
        share_of(outer_sum(normed, kv_grad_low)),
    )
    early, late_shares = lax.optimization_barrier((early, late_shares))
    late = lax.psum(late_shares, "ctx")
    down_grad, up_grad, out_grad = (part.astype(jnp.float32) for part in early)
    query_grad, keyvalue_grad = (part.astype(jnp.float32) for part in late)
    dnormed = times_transpose(dquery, w_query) * 0.125 + times_transpose(kv_grad_low, w_keyvalue)
    _, norm_pull_one = jax.vjp(normalize, hidden, gain_one, shift_one)
    dhidden_part, dgain_one, dshift_one = norm_pull_one(dnormed)
    input_grad = (dmiddle + dhidden_part).astype(jnp.bfloat16)
    (
        gain_one_grad,
        shift_one_grad,
        query_bias_grad,
        value_bias_grad,
        out_bias_grad,
        gain_two_grad,
        shift_two_grad,
        up_bias_grad,
        down_bias_grad,
    ) = sum_vectors(
        [
            dgain_one,
            dshift_one,
            jnp.sum(dquery.astype(jnp.float32), 0) * 0.125,
            jnp.sum(dvalue.astype(jnp.float32), 0),
            jnp.sum(dbranch.astype(jnp.float32), 0),
            dgain_two,
            dshift_two,
            jnp.sum(dpre.astype(jnp.float32), 0),
            jnp.sum(upstream, 0),
        ]
    )
    return (
        result.astype(jnp.bfloat16)[None],
        input_grad[None],
        gain_one_grad,
        shift_one_grad,
        query_grad,
        query_bias_grad,
        keyvalue_grad,
        value_bias_grad,
        out_grad,
        out_bias_grad,
        gain_two_grad,
        shift_two_grad,
        up_grad,
        up_bias_grad,
        down_grad,
        down_bias_grad,
    )


def solution(mesh):
    in_specs = (
        P("shard", "ctx", None),
        P("shard", "ctx", None),
        P(),
        P("shard"),
        P("shard"),
        P("shard", None),
        P("shard"),
        P("shard", None),
        P("shard"),
        P("shard", None),
        P("shard"),
        P("shard"),
        P("shard"),
        P("shard", None),
        P("shard"),
        P("shard", None),
        P("shard"),
    )
    out_specs = (
        P("shard", "ctx", None),
        P("shard", "ctx", None),
        P("shard"),
        P("shard"),
        P("shard", None),
        P("shard"),
        P("shard", None),
        P("shard"),
        P("shard", None),
        P("shard"),
        P("shard"),
        P("shard"),
        P("shard", None),
        P("shard"),
        P("shard", None),
        P("shard"),
    )
    return jax.shard_map(body, mesh=mesh, in_specs=in_specs, out_specs=out_specs, check_vma=False)
```

time: 985 us -> 772 us (0.78)
  waiting for transfers between devices: 717 us -> 416 us
  blocking collectives: 46.5 us -> 100 us
  local copies, waits for them, and re-layouts: 27.8 us -> 46.6 us
  other arithmetic: 21.3 us -> 32.1 us
    reduce_scatter x7 -> x6, waiting for transfers between devices: 357 us -> 57.9 us  [the longest x1 45.8 us: body(): lax.psum_scatter(jnp.concatenate([near_dk, near_dv], 1), 'ctx', scatter_d...]
    all_gather x1, waiting for transfers between devices: 170 us -> 65.7 us  [body(): lax.all_gather(near[:, lanes:], 'ctx', axis=0, axis_index_groups=far_grou...]
    psum x1 -> x2, waiting for transfers between devices: 181 us -> 271 us  [the longest x1 201 us: body(): early = lax.psum((down_share, up_share, out_share), 'ctx')]
    all_to_all x0 -> x3, blocking collectives: none -> 56.7 us  [the longest x2 34.4 us: to_heads(): lax.all_to_all(packed, 'ctx', 0, 0, axis_index_groups=near_groups(), tile...]
    unnamed x112 -> x143, local copies, waits for them, and re-layouts: 21.6 us -> 15.5 us
  transfers between devices with their start and end apart: 14 -> 15, of which waited for: 11 -> 8; matrix products, arithmetic and copies ran while one was open for 7% -> 12% of each run, Pallas kernels for 4% -> 5%
where the time goes in v2:
time: 772 us; the launch traced here: 762 us
  waiting for transfers between devices  416 us (54%)
  blocking collectives  100 us (13%)
  Pallas kernels  93.4 us (12%)
  matrix products  54.4 us (7%)
  local copies, waits for them, and re-layouts  46.6 us (6%)
  other arithmetic  32.1 us (4%)
  between operations  15.1 us (2%)
    psum x1, waiting for transfers between devices, body(): early = lax.psum((down_share, up_share, out_share), 'ctx')  201 us
    pallas_call x2, Pallas kernels, attention_call(): pl.pallas_call(kernel, out_shape=out_shape, grid_spec=pltpu.PrefetchScala...  93.4 us
    psum x1, waiting for transfers between devices, body(): late = lax.psum(late_shares, 'ctx')  70.5 us
    all_gather x1, waiting for transfers between devices, body(): lax.all_gather(near[:, lanes:], 'ctx', axis=0, axis_index_groups=far_grou...  65.7 us
    reduce_scatter x1, waiting for transfers between devices, body(): lax.psum_scatter(jnp.concatenate([near_dk, near_dv], 1), 'ctx', scatter_d...  45.8 us
    psum x1, blocking collectives, sum_vectors(): summed = lax.psum(packed, ('ctx', 'shard'))  41.8 us
    all_to_all x2, blocking collectives, to_heads(): lax.all_to_all(packed, 'ctx', 0, 0, axis_index_groups=near_groups(), tile...  34.4 us
    all_to_all x1, blocking collectives, to_tokens(): lax.all_to_all(packed, 'ctx', 0, 0, axis_index_groups=near_groups(), tile...  22.3 us
  transfers between devices with their start and end apart: 15, of which 8 were waited for; matrix products, arithmetic and copies ran while one was open for 12% of the time, Pallas kernels for 5%

profile of v2, /device:TPU:0, one launch (start us, length us, event | category | flops | bytes accessed | tf_op | source)
XLA Modules:
  0.0 762.2 jit_solution(9082953195908707433)
XLA Ops:
  25.4 9.8 %all-gather.11.cloned.1.call-done = bf16[768,1536]{1,0:T(8,128)(2,1)} async-done(((bf16[384,1536]{1,0:T(8,128)(2,1)}), bf16[768,1536]{1,0:T(8,128)(2,1)}) %all-gather.11.cloned.1.call-update) | async-done | bytes 2359312 | tf_op jit(solution)/shard_map/all_gather | solution.py:357
  39.7 23.1 %all_to_all.20 = bf16[4,288,576]{2,1,0:T(8,128)(2,1)S(1)} all-to-all(bf16[4,288,576]{2,1,0:T(8,128)(2,1)S(1)} %pad_maximum_fusion.1), channel_id=1, replica_groups={{0,2,4,6},{8,10,12,14},{16,18,20,22},{24,26,28,30},{1,3,5,7},{9,11,13,1..., dimensions={0} | all-to-all | bytes 2654208 | tf_op jit(solution)/shard_map/all_to_all | solution.py:280
  67.8 65.7 %all-gather.13.cloned.1.call-done = bf16[4608,384]{1,0:T(8,128)(2,1)} async-done(((bf16[1152,384]{1,0:T(8,128)(2,1)}), bf16[4608,384]{1,0:T(8,128)(2,1)}) %all-gather.13.cloned.1.call-update) | async-done | bytes 3538960 | tf_op jit(solution)/shard_map/all_gather | solution.py:372
  133.5 3.7 fusion.54
  137.2 39.6 %shard_map.288 = (f32[1152,192]{1,0:T(8,128)S(1)}, f32[8,432,128]{2,1,0:T(8,128)S(1)}) custom-call(s32[32]{0:T(128)S(1)} %reshape.276.table, s32[8]{0:T(128)S(1)} %reshape.277.mine, bf16[1152,192]{1,0:T(8,128)(2,1)S(1)} %copy-done.2, bf16[4608,192]{1,0:T(8,128)(2,1)S(1)} %get-tuple-element.63.k_ref, bf16[4608,192]{1,0:T(8,128)(2,1)S(1)} %get-tuple-element.62.v_ref), custom_call_target="tpu_custom_call" | custom-call | flops 2038431744 | bytes 7077888 | tf_op jit(solution)/shard_map/pallas_call | solution.py:225
  178.9 3.7 all-to-all-start.1
  183.5 7.8 %all-to-all-done.1 = bf16[4,288,192]{2,1,0:T(8,128)(2,1)S(1)} async-done(((bf16[4,288,192]{2,1,0:T(8,128)(2,1)}), bf16[4,288,192]{2,1,0:T(8,128)(2,1)S(1)}, u32[]{:S(2)}, u32[]{:S(2)}) %all-to-all-start.1) | async-done | bytes 442400 | tf_op jit(solution)/shard_map/all_to_all | solution.py:287
  194.8 5.8 convolution_add_fusion
  200.6 7.6 convert_reduce_fusion
  218.0 11.2 %all_to_all.21 = bf16[4,288,192]{2,1,0:T(8,128)(2,1)S(1)} all-to-all(bf16[4,288,192]{2,1,0:T(8,128)(2,1)S(1)} %bitcast.113), channel_id=1, replica_groups={{0,2,4,6},{8,10,12,14},{16,18,20,22},{24,26,28,30},{1,3,5,7},{9,11,13,1..., dimensions={0} | all-to-all | bytes 884736 | tf_op jit(solution)/shard_map/all_to_all | solution.py:280
  230.7 53.9 %shard_map.289 = (bf16[1152,192]{1,0:T(8,128)(2,1)S(1)}, bf16[4608,192]{1,0:T(8,128)(2,1)S(1)}, bf16[4608,192]{1,0:T(8,128)(2,1)S(1)}) custom-call(s32[32]{0:T(128)S(1)} %reshape.276.table, s32[8]{0:T(128)S(1)} %reshape.277.mine, bf16[1152,192]{1,0:T(8,128)(2,1)S(1)} %copy-done.3, bf16[1152,192]{1,0:T(8,128)(2,1)S(1)} %bitcast.101, ...), custom_call_target="tpu_custom_call" | custom-call | flops 5096079360 | bytes 7077888 | tf_op jit(solution)/shard_map/pallas_call | solution.py:225
  290.6 7.3 convolution_convert_fusion.1
  299.1 6.0 convolution_convert_fusion
  305.2 45.8 %reduce-scatter.7.cloned.1.call-done = bf16[1152,384]{1,0:T(8,128)(2,1)} async-done(((bf16[4608,384]{1,0:T(8,128)(2,1)}), bf16[1152,384]{1,0:T(8,128)(2,1)}) %reduce-scatter.7.cloned.1.call-update) | async-done | bytes 884752 | tf_op jit(solution)/shard_map/reduce_scatter | solution.py:398
  352.8 22.3 %all_to_all.22 = bf16[4,288,576]{2,1,0:T(8,128)(2,1)} all-to-all(bf16[4,288,576]{2,1,0:T(8,128)(2,1)S(1)} %bitcast.106), channel_id=1, replica_groups={{0,2,4,6},{8,10,12,14},{16,18,20,22},{24,26,28,30},{1,3,5,7},{9,11,13,1..., dimensions={0} | all-to-all | bytes 2654208 | tf_op jit(solution)/shard_map/all_to_all | solution.py:287
  375.1 3.1 copy.57
  386.8 4.1 convolution_convert_fusion.2
  391.1 5.1 reduce-scatter.11.cloned.1.call-done
  400.1 6.5 fusion.13
  415.7 7.0 reduce-scatter.17.cloned.1.call-done
  422.7 200.7 %all-reduce.8.cloned.1.call-done = (bf16[1536,768]{1,0:T(8,128)(2,1)}, bf16[384,3072]{1,0:T(8,128)(2,1)}, bf16[384,768]{1,0:T(8,128)(2,1)}) async-done(((bf16[1536,768]{1,0:T(8,128)(2,1)}, bf16[384,3072]{1,0:T(8,128)(2,1)}, bf16[384,768]{1,0:T(8,128)(2,1)}), (bf16[1536,768]{1,0:T(8,128)(2,1)}, bf16[384,3072]{1,0:T(8,128)(2,1)}, bf16[384,768]{1,0:T(8,128)(2,1)})) %all-reduce.8.cloned.1.call-update) | async-done | bytes 5308432 | tf_op jit(solution)/shard_map/psum | solution.py:394
  628.3 41.8 %psum.42 = f32[2,4608]{1,0:T(2,128)S(1)} all-reduce(f32[2,4608]{1,0:T(2,128)S(1)} %constant_dynamic-update-slice_fusion), channel_id=1, replica_groups=mesh['ctx'=16,'shard'=2] {'ctx','shard'}, use_global_device_ids=true, to_apply=%region_18.19 | all-reduce | flops 9216 | bytes 73728 | tf_op jit(solution)/shard_map/psum | solution.py:306
  672.5 4.6 convert_element_type.221
  679.7 70.5 %all-reduce.6.cloned.1.call-done = (bf16[384,768]{1,0:T(8,128)(2,1)}, bf16[384,1536]{1,0:T(8,128)(2,1)}) async-done(((bf16[384,768]{1,0:T(8,128)(2,1)}, bf16[384,1536]{1,0:T(8,128)(2,1)}), (bf16[384,768]{1,0:T(8,128)(2,1)}, bf16[384,1536]{1,0:T(8,128)(2,1)})) %all-reduce.6.cloned.1.call-update) | async-done | bytes 1769488 | tf_op jit(solution)/shard_map/psum | solution.py:412
  (258 shorter events, 90.5 us)
Async XLA Ops:
  7.2 15.7 %all-gather.9.cloned.1.call-start = ((), (), s32[]{:S(2)}) async-start(), calls=%async_computation.10 | async-start | bytes 1769472 | tf_op jit(solution)/shard_map/all_gather | solution.py:358
  7.9 27.3 %all-gather.11.cloned.1.call-start = ((), (), s32[]{:S(2)}) async-start(), calls=%async_computation.11 | async-start | bytes 3538944 | tf_op jit(solution)/shard_map/all_gather | solution.py:357
  8.7 124.8 %all-gather.13.cloned.1.call-start = ((), (), s32[]{:S(2)}) async-start(), calls=%async_computation.12 | async-start | bytes 4423680 | tf_op jit(solution)/shard_map/all_gather | solution.py:372
  64.1 128.2 %all-gather.15.cloned.1.call-start = ((), (), s32[]{:S(2)}) async-start(), calls=%async_computation.13 | async-start | bytes 1769472 | tf_op jit(solution)/shard_map/all_gather | solution.py:360
  64.7 130.0 %all-gather.17.cloned.1.call-start = ((), (), s32[]{:S(2)}) async-start(), calls=%async_computation.14 | async-start | bytes 7077888 | tf_op jit(solution)/shard_map/all_gather | solution.py:361
  65.3 135.3 %all-gather.19.cloned.1.call-start = ((), (), s32[]{:S(2)}) async-start(), calls=%async_computation.15 | async-start | bytes 7077888 | tf_op jit(solution)/shard_map/all_gather | solution.py:359
  137.2 39.6 %copy-start = (bf16[4608,192]{1,0:T(8,128)(2,1)}, bf16[4608,192]{1,0:T(8,128)(2,1)S(1)}, u32[]{:S(2)}) copy-start(bf16[4608,192]{1,0:T(8,128)(2,1)S(1)} %get-tuple-element.62.v_ref) | copy-start | bytes 5308420
  137.2 39.6 %copy-start.1 = (bf16[4608,192]{1,0:T(8,128)(2,1)}, bf16[4608,192]{1,0:T(8,128)(2,1)S(1)}, u32[]{:S(2)}) copy-start(bf16[4608,192]{1,0:T(8,128)(2,1)S(1)} %get-tuple-element.63.k_ref) | copy-start | bytes 5308420
  178.9 12.4 %all-to-all-start.1 = ((bf16[4,288,192]{2,1,0:T(8,128)(2,1)}), bf16[4,288,192]{2,1,0:T(8,128)(2,1)S(1)}, u32[]{:S(2)}, u32[]{:S(2)}) async-start(bf16[4,288,192]{2,1,0:T(8,128)(2,1)} %bitcast.5), calls=%async_computation.1 | async-start | bytes 1179648 | tf_op jit(solution)/shard_map/all_to_all | solution.py:287
  182.6 168.4 %reduce-scatter.7.cloned.1.call-start = ((), (), s32[]{:S(2)}) async-start(), calls=%async_computation.16 | async-start | bytes 4423680 | tf_op jit(solution)/shard_map/reduce_scatter | solution.py:398
  287.6 103.4 %reduce-scatter.13.cloned.1.call-start = ((), (), s32[]{:S(2)}) async-start(), calls=%async_computation.19 | async-start | bytes 1769472 | tf_op jit(solution)/shard_map/reduce_scatter | solution.py:316
  290.6 100.5 %reduce-scatter.9.cloned.1.call-start = ((), (), s32[]{:S(2)}) async-start(), calls=%async_computation.17 | async-start | bytes 7077888 | tf_op jit(solution)/shard_map/reduce_scatter | solution.py:316
  298.0 98.2 %reduce-scatter.11.cloned.1.call-start = ((), (), s32[]{:S(2)}) async-start(), calls=%async_computation.18 | async-start | bytes 7077888 | tf_op jit(solution)/shard_map/reduce_scatter | solution.py:316
  305.2 110.5 %reduce-scatter.15.cloned.1.call-start = ((), (), s32[]{:S(2)}) async-start(), calls=%async_computation.20 | async-start | bytes 1769472 | tf_op jit(solution)/shard_map/reduce_scatter | solution.py:316
  382.4 40.3 %reduce-scatter.17.cloned.1.call-start = ((), (), s32[]{:S(2)}) async-start(), calls=%async_computation.21 | async-start | bytes 3538944 | tf_op jit(solution)/shard_map/reduce_scatter | solution.py:316
  391.0 232.4 %all-reduce.8.cloned.1.call-start = ((), (), s32[]{:S(2)}) async-start(), calls=%async_computation.23 | async-start | bytes 10616832 | tf_op jit(solution)/shard_map/psum | solution.py:394
  396.2 354.0 %all-reduce.6.cloned.1.call-start = ((), (), s32[]{:S(2)}) async-start(), calls=%async_computation.22 | async-start | bytes 3538944 | tf_op jit(solution)/shard_map/psum | solution.py:412
  409.8 215.9 %copy-start.11 = (f32[288,768]{1,0:T(8,128)S(1)}, f32[288,768]{1,0:T(8,128)}, u32[]{:S(2)}) copy-start(f32[288,768]{1,0:T(8,128)} %copy-done.10) | copy-start | bytes 2654212
  415.7 212.5 %copy-start.49 = (f32[2,384]{1,0:T(2,128)S(1)}, f32[2,384]{1,0:T(2,128)}, u32[]{:S(2)}) copy-start(f32[2,384]{1,0:T(2,128)} %reshape.288) | copy-start | bytes 9220
  415.7 212.5 %copy-start.50 = (f32[2,384]{1,0:T(2,128)S(1)}, f32[2,384]{1,0:T(2,128)}, u32[]{:S(2)}) copy-start(f32[2,384]{1,0:T(2,128)} %reshape.289) | copy-start | bytes 9220
  415.7 212.5 %copy-start.48 = (f32[2,384]{1,0:T(2,128)S(1)}, f32[2,384]{1,0:T(2,128)}, u32[]{:S(2)}) copy-start(f32[2,384]{1,0:T(2,128)} %reshape.291) | copy-start | bytes 9220
  415.7 212.5 %copy-start.46 = (f32[2,384]{1,0:T(2,128)S(1)}, f32[2,384]{1,0:T(2,128)}, u32[]{:S(2)}) copy-start(f32[2,384]{1,0:T(2,128)} %reshape.292) | copy-start | bytes 9220
  415.7 212.6 %copy-start.47 = (f32[2,384]{1,0:T(2,128)S(1)}, f32[2,384]{1,0:T(2,128)}, u32[]{:S(2)}) copy-start(f32[2,384]{1,0:T(2,128)} %reshape.293) | copy-start | bytes 9220
  623.4 48.1 %copy-start.21 = (bf16[384,768]{1,0:T(8,128)(2,1)S(1)}, bf16[384,768]{1,0:T(8,128)(2,1)}, u32[]{:S(2)}) copy-start(bf16[384,768]{1,0:T(8,128)(2,1)} %get-tuple-element.33) | copy-start | bytes 1769476
  (53 other events, 347.9 us)
Sparse Core Ops, SparseCore 0:
  9.6 11.9 all-gather.8
  23.1 12.1 all-gather.10
  64.3 69.1 all-gather.12
  134.9 7.8 all-gather.14
  144.1 15.5 all-gather.16
  161.1 15.6 all-gather.18
  287.7 63.1 reduce-scatter.6
  353.8 8.9 reduce-scatter.12
  365.8 13.7 reduce-scatter.8
  382.3 13.7 reduce-scatter.10
  399.1 9.8 reduce-scatter.14
  411.6 11.0 reduce-scatter.16
  430.3 193.0 all-reduce.7
  629.0 121.1 all-reduce.5
